TPU v7x, 32 devices: a whole 2x2x4 slice. The times are simulated.
32 devices in a mesh: slot: 4 (over z), ctx: 2 (over x), tp: 4 (over y, core).
Axes of the slice: x: 2, y: 2, z: 4, core: 2. Of those that a mesh axis runs over, the one named last changes fastest.
Arguments:
- inputs: bfloat16 [4, 1024, 2048], P('slot', 'ctx'), may hold values from -6 to 6
- lengths: int32 [4], P('slot'), may hold values from 256 to 1024, as said below
- ln_gain: float32 [2, 2048], replicated, may hold values from 0.5 to 1.5
- ln_shift: float32 [2, 2048], replicated, may hold values from -3 to 3
- w_qkv: bfloat16 [2, 3, 2048, 2048], P(None, None, ('slot', 'ctx'), 'tp'), may hold values from -0.125 to 0.125
- b_qkv: float32 [2, 3, 2048], P(None, None, 'tp'), may hold values from -2 to 2
- w_out: bfloat16 [2, 2048, 2048], P(None, 'tp', ('slot', 'ctx')), may hold values from -0.75 to 0.75
- b_out: float32 [2, 2048], replicated, may hold values from -2 to 2
- w_up: bfloat16 [2, 2048, 8192], P(None, ('slot', 'ctx'), 'tp'), may hold values from -0.125 to 0.125
- b_up: float32 [2, 8192], P(None, 'tp'), may hold values from -3 to 3
- w_down: bfloat16 [2, 8192, 2048], P(None, 'tp', ('slot', 'ctx')), may hold values from -0.0625 to 0.0625
- b_down: float32 [2, 2048], replicated, may hold values from -2 to 2
- cotangent: bfloat16 [4, 1024, 2048], P('slot', 'ctx'), may hold values from -6 to 6
Outputs:
- block_out: bfloat16 [4, 1024, 2048], P('slot', 'ctx')
- grad_input: bfloat16 [4, 1024, 2048], P('slot', 'ctx')
- grad_ln_gain: float32 [2, 2048], replicated
- grad_ln_shift: float32 [2, 2048], replicated
- grad_w_qkv: float32 [2, 3, 2048, 2048], P(None, None, ('slot', 'ctx'), 'tp')
- grad_b_qkv: float32 [2, 3, 2048], P(None, None, 'tp')
- grad_w_out: float32 [2, 2048, 2048], P(None, 'tp', ('slot', 'ctx'))
- grad_b_out: float32 [2, 2048], replicated
- grad_w_up: float32 [2, 2048, 8192], P(None, ('slot', 'ctx'), 'tp')
- grad_b_up: float32 [2, 8192], P(None, 'tp')
- grad_w_down: float32 [2, 8192, 2048], P(None, 'tp', ('slot', 'ctx'))
- grad_b_down: float32 [2, 2048], replicated
Inputs may be any that keep to these rules, and one draw needn't show every extreme that they name: `lengths`: valid positions of a slot are a prefix of it; in every draw one slot, drawn from the seed, is full.
All inputs are finite; a program needn't handle non-finite values.
Results may differ from a plain program's by a relative error of at most 0.033.
Values may be sent and summed in bfloat16 or wider, within the bound.
No kernel may reach another device: no remote copies, remote signals or barrier semaphores. Data moves between devices by JAX's collectives and lax.ppermute only.
A program may use at most 320 MiB of HBM per device.

v0:
```python
import math

import jax
import jax.numpy as jnp
from jax import lax
from jax.sharding import PartitionSpec as P

HD = 64
ROT = 32
LAYERS = 2


masked = -1e30


def layer_norm(hidden, gain, shift):
    centre = jnp.mean(hidden, -1, keepdims=True)
    centred = hidden - centre
    variance = jnp.mean(centred * centred, -1, keepdims=True)
    return centred * lax.rsqrt(variance + 1e-05) * gain + shift


def gelu_tanh(value):
    inner = 0.7978845608028654 * (value + 0.044715 * value * value * value)
    return 0.5 * value * (1.0 + jnp.tanh(inner))


def rotary_tables(positions):
    half_rot = ROT // 2
    freqs = jnp.exp(jnp.arange(half_rot, dtype=jnp.float32) * (-2.0 * math.log(10000.0) / ROT))
    angles = positions.astype(jnp.float32)[:, None] * freqs[None, :]
    return (jnp.cos(angles), jnp.sin(angles))


def rotate(tensor, cosine, sine):
    half_rot = ROT // 2
    lead_part = tensor[..., :half_rot]
    tail_part = tensor[..., half_rot:ROT]
    remain_part = tensor[..., ROT:]
    cos_rows = cosine[:, None, :]
    sin_rows = sine[:, None, :]
    return jnp.concatenate(
        [
            lead_part * cos_rows - tail_part * sin_rows,
            tail_part * cos_rows + lead_part * sin_rows,
            remain_part,
        ],
        axis=-1,
    )


def block_scores(query, keys, start, block, positions, length):
    key_block = lax.dynamic_slice_in_dim(keys, start, block, 0)
    scores = jnp.einsum(
        "qhd,khd->hqk", query, key_block, preferred_element_type=jnp.float32
    ) * HD ** (-0.5)
    key_pos = start + jnp.arange(block, dtype=jnp.int32)
    allowed = (key_pos[None, :] <= positions[:, None]) & (key_pos[None, :] < length)
    return jnp.where(allowed[None], scores, masked)


def attend_forward(query, keys, values, positions, length):
    slot_len = keys.shape[0]
    block = math.gcd(512, slot_len)
    count = slot_len // block
    rows, heads_here = (query.shape[0], query.shape[1])

    def stats_update(block_idx, carry):
        row_top, total = carry
        scores = block_scores(query, keys, block_idx * block, block, positions, length)
        new_top = jnp.maximum(row_top, jnp.max(scores, -1))
        total = total * jnp.exp(row_top - new_top) + jnp.sum(
            jnp.exp(scores - new_top[..., None]), -1
        )
        return (new_top, total)

    start_stats = (
        jnp.full((heads_here, rows), masked, jnp.float32),
        jnp.zeros((heads_here, rows), jnp.float32),
    )
    row_top, total = lax.fori_loop(0, count, stats_update, start_stats)
    logsum = row_top + jnp.log(total)

    def output_update(block_idx, accum):
        start = block_idx * block
        scores = block_scores(query, keys, start, block, positions, length)
        probs = jnp.exp(scores - logsum[..., None]).astype(jnp.bfloat16)
        value_block = lax.dynamic_slice_in_dim(values, start, block, 0)
        return accum + jnp.einsum(
            "hqk,khd->qhd", probs, value_block, preferred_element_type=jnp.float32
        )

    result = lax.fori_loop(0, count, output_update, jnp.zeros((rows, heads_here, HD), jnp.float32))
    return (result, logsum)


def attend_backward(query, keys, values, positions, length, logsum, result, grad_out):
    slot_len = keys.shape[0]
    block = math.gcd(512, slot_len)
    count = slot_len // block
    delta = jnp.sum(grad_out.astype(jnp.float32) * result, -1).T

    def grad_update(block_idx, carry):
        grad_query, grad_keys, grad_values = carry
        start = block_idx * block
        scores = block_scores(query, keys, start, block, positions, length)
        probs = jnp.exp(scores - logsum[..., None])
        key_block = lax.dynamic_slice_in_dim(keys, start, block, 0)
        value_block = lax.dynamic_slice_in_dim(values, start, block, 0)
        grad_probs = jnp.einsum(
            "qhd,khd->hqk", grad_out, value_block, preferred_element_type=jnp.float32
        )
        grad_scores = (probs * (grad_probs - delta[..., None]) * HD ** (-0.5)).astype(jnp.bfloat16)
        grad_query = grad_query + jnp.einsum(
            "hqk,khd->qhd", grad_scores, key_block, preferred_element_type=jnp.float32
        )
        key_term = jnp.einsum(
            "hqk,qhd->khd", grad_scores, query, preferred_element_type=jnp.float32
        )
        value_term = jnp.einsum(
            "hqk,qhd->khd", probs.astype(jnp.bfloat16), grad_out, preferred_element_type=jnp.float32
        )
        grad_keys = lax.dynamic_update_slice_in_dim(grad_keys, key_term, start, 0)
        grad_values = lax.dynamic_update_slice_in_dim(grad_values, value_term, start, 0)
        return (grad_query, grad_keys, grad_values)

    zero_keys = jnp.zeros(keys.shape, jnp.float32)
    start_grads = (jnp.zeros(query.shape, jnp.float32), zero_keys, zero_keys)
    return lax.fori_loop(0, count, grad_update, start_grads)


def on_device(
    inputs,
    lengths,
    ln_gain,
    ln_shift,
    w_qkv,
    b_qkv,
    w_out,
    b_out,
    w_up,
    b_up,
    w_down,
    b_down,
    cotangent,
):
    slots_here, run, width = inputs.shape
    slot_len = run * lax.axis_size("ctx")
    heads_here = w_qkv.shape[3] // HD
    tokens = slots_here * run
    run_start = lax.axis_index("ctx") * run
    positions = run_start + jnp.arange(run, dtype=jnp.int32)
    cosine, sine = rotary_tables(positions)
    cosine = jnp.tile(cosine, (slots_here, 1))
    sine = jnp.tile(sine, (slots_here, 1))
    valid = (positions[None, :] < lengths[:, None]).astype(jnp.float32).reshape(tokens, 1)
    hidden = inputs.reshape(tokens, width).astype(jnp.float32)
    saved = []
    for layer_idx in range(LAYERS):
        weights = (
            lax.all_gather(w_qkv[layer_idx], ("slot", "ctx"), axis=1, tiled=True),
            lax.all_gather(w_out[layer_idx], ("slot", "ctx"), axis=1, tiled=True),
            lax.all_gather(w_up[layer_idx], ("slot", "ctx"), axis=0, tiled=True),
            lax.all_gather(w_down[layer_idx], ("slot", "ctx"), axis=1, tiled=True),
        )
        qkv_full, out_full, up_full, down_full = weights
        normed = layer_norm(hidden, ln_gain[layer_idx], ln_shift[layer_idx]).astype(jnp.bfloat16)
        projected = (
            jnp.einsum("td,pde->pte", normed, qkv_full, preferred_element_type=jnp.float32)
            + b_qkv[layer_idx][:, None, :]
        )
        query = rotate(projected[0].reshape(tokens, heads_here, HD), cosine, sine).astype(
            jnp.bfloat16
        )
        key_local = rotate(projected[1].reshape(tokens, heads_here, HD), cosine, sine).astype(
            jnp.bfloat16
        )
        value_local = projected[2].astype(jnp.bfloat16)
        keys_all, values_all = (
            lax.all_gather(key_local.reshape(slots_here, run, -1), "ctx", axis=1, tiled=True),
            lax.all_gather(value_local.reshape(slots_here, run, -1), "ctx", axis=1, tiled=True),
        )
        logsums = []
        slot_idx = 0
        slot_keys = keys_all[slot_idx].reshape(slot_len, heads_here, HD)
        slot_values = values_all[slot_idx].reshape(slot_len, heads_here, HD)
        result, logsum = attend_forward(query, slot_keys, slot_values, positions, lengths[slot_idx])
        logsums.append(logsum)
        result_all = result
        attended = result_all.reshape(tokens, -1).astype(jnp.bfloat16)
        upward = jnp.dot(normed, up_full, preferred_element_type=jnp.float32) + b_up[layer_idx]
        activated = gelu_tanh(upward).astype(jnp.bfloat16)
        partial_sum = jnp.dot(attended, out_full, preferred_element_type=jnp.float32) + jnp.dot(
            activated, down_full, preferred_element_type=jnp.float32
        )
        branch = lax.psum(partial_sum.astype(jnp.bfloat16), "tp").astype(jnp.float32)
        kept_weights = None
        saved.append(
            (
                hidden,
                normed,
                query,
                keys_all,
                values_all,
                result_all,
                logsums,
                attended,
                upward,
                activated,
                kept_weights,
            )
        )
        hidden = hidden + branch + b_out[layer_idx] + b_down[layer_idx]
    block_out = (hidden * valid).astype(jnp.bfloat16).reshape(inputs.shape)
    grad_hidden = cotangent.reshape(tokens, width).astype(jnp.float32) * valid
    layer_grads = []
    for layer_idx in reversed(range(LAYERS)):
        (
            layer_in,
            normed,
            query,
            keys_all,
            values_all,
            result_all,
            logsums,
            attended,
            upward,
            activated,
            kept_weights,
        ) = saved[layer_idx]
        qkv_full, out_full, up_full, down_full = (
            lax.all_gather(w_qkv[layer_idx], ("slot", "ctx"), axis=1, tiled=True),
            lax.all_gather(w_out[layer_idx], ("slot", "ctx"), axis=1, tiled=True),
            lax.all_gather(w_up[layer_idx], ("slot", "ctx"), axis=0, tiled=True),
            lax.all_gather(w_down[layer_idx], ("slot", "ctx"), axis=1, tiled=True),
        )
        grad_branch = grad_hidden.astype(jnp.bfloat16)
        grad_out_w = jnp.einsum(
            "ta,tb->ab", attended, grad_branch, preferred_element_type=jnp.float32
        )
        grad_down_w = jnp.einsum(
            "tf,tb->fb", activated, grad_branch, preferred_element_type=jnp.float32
        )
        grad_bias_out = jnp.sum(grad_hidden, 0)
        grad_attended = jnp.einsum(
            "tb,ab->ta", grad_branch, out_full, preferred_element_type=jnp.float32
        ).astype(jnp.bfloat16)
        grad_activated = jnp.einsum(
            "tb,fb->tf", grad_branch, down_full, preferred_element_type=jnp.float32
        )
        gelu_value, gelu_pull = jax.vjp(gelu_tanh, upward)
        grad_upward = gelu_pull(grad_activated)[0].astype(jnp.bfloat16)
        grad_attended_heads = grad_attended.reshape(tokens, heads_here, HD)
        slot_idx = 0
        slot_keys = keys_all[slot_idx].reshape(slot_len, heads_here, HD)
        slot_values = values_all[slot_idx].reshape(slot_len, heads_here, HD)
        grad_query, grad_keys, grad_values = attend_backward(
            query,
            slot_keys,
            slot_values,
            positions,
            lengths[slot_idx],
            logsums[slot_idx],
            result_all,
            grad_attended_heads,
        )
        key_grads = [grad_keys.reshape(slot_len, -1)]
        value_grads = [grad_values.reshape(slot_len, -1)]
        grad_keys_own, grad_values_own = (
            lax.psum_scatter(
                jnp.stack(key_grads).astype(jnp.bfloat16), "ctx", scatter_dimension=1, tiled=True
            ).astype(jnp.float32),
            lax.psum_scatter(
                jnp.stack(value_grads).astype(jnp.bfloat16), "ctx", scatter_dimension=1, tiled=True
            ).astype(jnp.float32),
        )
        grad_q_lin = rotate(grad_query, cosine, -sine).reshape(tokens, -1).astype(jnp.bfloat16)
        grad_k_lin = (
            rotate(grad_keys_own.reshape(tokens, heads_here, HD), cosine, -sine)
            .reshape(tokens, -1)
            .astype(jnp.bfloat16)
        )
        grad_v_lin = grad_values_own.reshape(tokens, -1).astype(jnp.bfloat16)
        grad_proj = jnp.stack([grad_q_lin, grad_k_lin, grad_v_lin])
        grad_qkv_w = jnp.einsum(
            "td,pte->pde", normed, grad_proj, preferred_element_type=jnp.float32
        )
        grad_bias_qkv = jnp.sum(grad_proj.astype(jnp.float32), 1)
        grad_up_w = jnp.einsum("td,tf->df", normed, grad_upward, preferred_element_type=jnp.float32)
        grad_bias_up = jnp.sum(grad_upward.astype(jnp.float32), 0)
        grad_normed = jnp.einsum(
            "pte,pde->td", grad_proj, qkv_full, preferred_element_type=jnp.float32
        )
        grad_normed = grad_normed + jnp.einsum(
            "tf,df->td", grad_upward, up_full, preferred_element_type=jnp.float32
        )
        grad_normed = lax.psum(grad_normed.astype(jnp.bfloat16), "tp").astype(jnp.float32)
        norm_value, norm_pull = jax.vjp(
            layer_norm, layer_in, ln_gain[layer_idx], ln_shift[layer_idx]
        )
        grad_in, grad_gain, grad_shift = norm_pull(grad_normed)
        grad_hidden = grad_hidden + grad_in
        weight_sums = (
            lax.psum_scatter(
                grad_qkv_w.astype(jnp.bfloat16), ("slot", "ctx"), scatter_dimension=1, tiled=True
            ).astype(jnp.float32),
            lax.psum_scatter(
                grad_out_w.astype(jnp.bfloat16), ("slot", "ctx"), scatter_dimension=1, tiled=True
            ).astype(jnp.float32),
            lax.psum_scatter(
                grad_up_w.astype(jnp.bfloat16), ("slot", "ctx"), scatter_dimension=0, tiled=True
            ).astype(jnp.float32),
            lax.psum_scatter(
                grad_down_w.astype(jnp.bfloat16), ("slot", "ctx"), scatter_dimension=1, tiled=True
            ).astype(jnp.float32),
        )
        small_sums = (
            lax.psum(grad_gain.astype(jnp.bfloat16), ("slot", "ctx")).astype(jnp.float32),
            lax.psum(grad_shift.astype(jnp.bfloat16), ("slot", "ctx")).astype(jnp.float32),
            lax.psum(grad_bias_qkv.astype(jnp.bfloat16), ("slot", "ctx")).astype(jnp.float32),
            lax.psum(grad_bias_out.astype(jnp.bfloat16), ("slot", "ctx")).astype(jnp.float32),
            lax.psum(grad_bias_up.astype(jnp.bfloat16), ("slot", "ctx")).astype(jnp.float32),
        )
        layer_grads.insert(0, (weight_sums, small_sums))
    grad_input = grad_hidden.astype(jnp.bfloat16).reshape(inputs.shape)
    grad_ln_gain = jnp.stack([entry[1][0] for entry in layer_grads])
    grad_ln_shift = jnp.stack([entry[1][1] for entry in layer_grads])
    grad_w_qkv = jnp.stack([entry[0][0] for entry in layer_grads])
    grad_b_qkv = jnp.stack([entry[1][2] for entry in layer_grads])
    grad_w_out = jnp.stack([entry[0][1] for entry in layer_grads])
    grad_b_out = jnp.stack([entry[1][3] for entry in layer_grads])
    grad_w_up = jnp.stack([entry[0][2] for entry in layer_grads])
    grad_b_up = jnp.stack([entry[1][4] for entry in layer_grads])
    grad_w_down = jnp.stack([entry[0][3] for entry in layer_grads])
    return (
        block_out,
        grad_input,
        grad_ln_gain,
        grad_ln_shift,
        grad_w_qkv,
        grad_b_qkv,
        grad_w_out,
        grad_b_out,
        grad_w_up,
        grad_b_up,
        grad_w_down,
        grad_b_out,
    )


def solution(mesh):
    return jax.shard_map(
        on_device,
        mesh=mesh,
        in_specs=(
            P("slot", "ctx", None),
            P("slot"),
            P(),
            P(),
            P(None, None, ("slot", "ctx"), "tp"),
            P(None, None, "tp"),
            P(None, "tp", ("slot", "ctx")),
            P(),
            P(None, ("slot", "ctx"), "tp"),
            P(None, "tp"),
            P(None, "tp", ("slot", "ctx")),
            P(),
            P("slot", "ctx", None),
        ),
        out_specs=(
            P("slot", "ctx", None),
            P("slot", "ctx", None),
            P(),
            P(),
            P(None, None, ("slot", "ctx"), "tp"),
            P(None, None, "tp"),
            P(None, "tp", ("slot", "ctx")),
            P(),
            P(None, ("slot", "ctx"), "tp"),
            P(None, "tp"),
            P(None, "tp", ("slot", "ctx")),
            P(),
        ),
        check_vma=False,
    )
```

profile of v0, /device:TPU:0, one launch (start us, length us, event | category | flops | bytes accessed | tf_op | source)
XLA Modules:
  0.0 2297.1 jit_solution(12820518274293453526)
XLA Ops:
  13.1 100.7 %all-gather.29.cloned.1.call-done = bf16[1,3,2048,512]{2,3,1,0:T(8,128)(2,1)} async-done(((bf16[1,3,256,512]{2,3,1,0:T(8,128)(2,1)}), bf16[1,3,2048,512]{2,3,1,0:T(8,128)(2,1)}) %all-gather.29.cloned.1.call-update) | async-done | bytes 6291472 | tf_op jit(solution)/shard_map/all_gather | solution.py:161
  141.9 24.3 %while.96 = (s32[]{:T(128)}, f32[8,512]{1,0:T(8,128)S(1)}, f32[8,512]{1,0:T(8,128)S(1)}, s32[]{:T(128)}, bf16[1024,8,64]{0,2,1:T(8,128)(2,1)}, /*index=5*/bf16[5...) while((s32[]{:T(128)}, f32[8,512]{1,0:T(8,128)S(1)}, ...), condition=%wide.region_5.6_spmd.clone, body=%wide.region_2.5_spmd.clone.sunk | while | flops 283662336 | bytes 18834616 | solution.py:81
  182.7 110.2 %all-gather.33.cloned.1.call-done = bf16[1,2048,2048]{2,1,0:T(8,128)(2,1)} async-done(((bf16[1,256,2048]{2,1,0:T(8,128)(2,1)}), bf16[1,2048,2048]{2,1,0:T(8,128)(2,1)}) %all-gather.33.cloned.1.call-update) | async-done | bytes 8388624 | tf_op jit(solution)/shard_map/all_gather | solution.py:163
  302.7 116.2 %all-gather.35.cloned.1.call-done = bf16[1,2048,2048]{2,1,0:T(8,128)(2,1)} async-done(((bf16[1,2048,256]{2,1,0:T(8,128)(2,1)}), bf16[1,2048,2048]{2,1,0:T(8,128)(2,1)}) %all-gather.35.cloned.1.call-update) | async-done | bytes 8388624 | tf_op jit(solution)/shard_map/all_gather | solution.py:164
  430.6 39.6 %all-gather.31.cloned.1.call-done = bf16[1,512,2048]{2,1,0:T(8,128)(2,1)} async-done(((bf16[1,512,256]{2,1,0:T(8,128)(2,1)}), bf16[1,512,2048]{2,1,0:T(8,128)(2,1)}) %all-gather.31.cloned.1.call-update) | async-done | bytes 2097168 | tf_op jit(solution)/shard_map/all_gather | solution.py:162
  478.2 47.2 %all-reduce.6.cloned.1.call-done = bf16[512,2048]{1,0:T(8,128)(2,1)} async-done(((bf16[512,2048]{1,0:T(8,128)(2,1)}), bf16[512,2048]{1,0:T(8,128)(2,1)}) %all-reduce.6.cloned.1.call-update) | async-done | bytes 2097168 | tf_op jit(solution)/shard_map/psum | solution.py:196
  532.2 96.1 %all-gather.37.cloned.1.call-done = bf16[1,3,2048,512]{2,3,1,0:T(8,128)(2,1)} async-done(((bf16[1,3,256,512]{2,3,1,0:T(8,128)(2,1)}), bf16[1,3,2048,512]{2,3,1,0:T(8,128)(2,1)}) %all-gather.37.cloned.1.call-update) | async-done | bytes 6291472 | tf_op jit(solution)/shard_map/all_gather | solution.py:161
  656.7 24.7 %while.98 = (s32[]{:T(128)}, f32[8,512]{1,0:T(8,128)S(1)}, f32[8,512]{1,0:T(8,128)S(1)}, s32[]{:T(128)}, bf16[1024,8,64]{0,2,1:T(8,128)(2,1)}, /*index=5*/bf16[5...) while((s32[]{:T(128)}, f32[8,512]{1,0:T(8,128)S(1)}, ...), condition=%wide.region_14.15_spmd.clone, body=%wide.region_11.14_spmd.clone.sunk | while | flops 283662336 | bytes 18834616 | solution.py:81
  695.4 38.0 %all-gather.39.cloned.1.call-done = bf16[1,512,2048]{2,1,0:T(8,128)(2,1)} async-done(((bf16[1,512,256]{2,1,0:T(8,128)(2,1)}), bf16[1,512,2048]{2,1,0:T(8,128)(2,1)}) %all-gather.39.cloned.1.call-update) | async-done | bytes 2097168 | tf_op jit(solution)/shard_map/all_gather | solution.py:162
  740.7 38.5 %while.100 = (s32[]{:T(128)}, f32[512,8,64]{0,2,1:T(8,128)S(1)}, bf16[1024,8,64]{0,2,1:T(8,128)(2,1)}, bf16[1024,8,64]{0,2,1:T(8,128)(2,1)}, bf16[1024,8,64]{0,2...) while((s32[]{:T(128)}, f32[512,8,64]{0,2,1:T(8,128)S(1)}, ...), condition=%wide.region_20.21_spmd.clone, body=%wide.region_19.20_spmd.clone.sunk | while | flops 1366296576 | bytes 100984136 | solution.py:129
  779.3 79.4 %all-gather.41.cloned.1.call-done = bf16[1,2048,2048]{2,1,0:T(8,128)(2,1)} async-done(((bf16[1,256,2048]{2,1,0:T(8,128)(2,1)}), bf16[1,2048,2048]{2,1,0:T(8,128)(2,1)}) %all-gather.41.cloned.1.call-update) | async-done | bytes 8388624 | tf_op jit(solution)/shard_map/all_gather | solution.py:163
  871.6 113.5 %all-gather.43.cloned.1.call-done = bf16[1,2048,2048]{2,1,0:T(8,128)(2,1)} async-done(((bf16[1,2048,256]{2,1,0:T(8,128)(2,1)}), bf16[1,2048,2048]{2,1,0:T(8,128)(2,1)}) %all-gather.43.cloned.1.call-update) | async-done | bytes 8388624 | tf_op jit(solution)/shard_map/all_gather | solution.py:164
  1010.6 18.3 reduce-scatter.15.cloned.1.call-done
  1037.9 51.5 %all-reduce.8.cloned.1.call-done = bf16[512,2048]{1,0:T(8,128)(2,1)} async-done(((bf16[512,2048]{1,0:T(8,128)(2,1)}), bf16[512,2048]{1,0:T(8,128)(2,1)}) %all-reduce.8.cloned.1.call-update) | async-done | bytes 2097168 | tf_op jit(solution)/shard_map/psum | solution.py:297
  1108.4 43.1 %while.101 = (s32[]{:T(128)}, f32[512,8,64]{0,2,1:T(8,128)}, bf16[1024,8,64]{0,2,1:T(8,128)(2,1)}, bf16[1024,8,64]{0,2,1:T(8,128)(2,1)}, bf16[1024,8,64]{0,2,1:T...) while((s32[]{:T(128)}, f32[512,8,64]{0,2,1:T(8,128)}, ...), condition=%wide.region_28.29_spmd.clone, body=%wide.region_27.28_spmd.clone.sunk | while | flops 1366296576 | bytes 105178488 | solution.py:129
  1298.1 38.9 %all-reduce = (bf16[1,2048]{1,0:T(2,128)(2,1)S(1)}, bf16[1,2048]{1,0:T(2,128)(2,1)S(1)}, bf16[1,2048]{1,0:T(2,128)(2,1)S(1)}, bf16[1,2048]{1,0:T(2,128)(2,1)S(1)...) all-reduce(bf16[1,2048]{1,0:T(2,128)(2,1)S(1)} %stack.141, ...), channel_id=1, replica_groups=mesh['slot'=4,'ctx'=2,'tp'=4] {'slot','ctx'}, use_global_device_ids=true, to_apply=%region_37.38 | all-reduce | flops 19456 | bytes 77824 | tf_op jit(solution)/shard_map/psum | solution.py:318
  1346.5 17.1 reduce-scatter.27.cloned.1.call-done
  1363.6 71.0 %reduce-scatter.25.cloned.1.call-done = bf16[512,256]{1,0:T(8,128)(2,1)} async-done(((bf16[512,2048]{1,0:T(8,128)(2,1)}), bf16[512,256]{1,0:T(8,128)(2,1)}) %reduce-scatter.25.cloned.1.call-update) | async-done | bytes 262160 | tf_op jit(solution)/shard_map/reduce_scatter | solution.py:307
  1436.7 119.3 %reduce-scatter.23.cloned.1.call-done = bf16[3,256,512]{1,2,0:T(8,128)(2,1)} async-done(((bf16[3,2048,512]{1,2,0:T(8,128)(2,1)}), bf16[3,256,512]{1,2,0:T(8,128)(2,1)}) %reduce-scatter.23.cloned.1.call-update) | async-done | bytes 786448 | tf_op jit(solution)/shard_map/reduce_scatter | solution.py:304
  1556.0 121.6 %reduce-scatter.21.cloned.1.call-done = bf16[3,256,512]{1,2,0:T(8,128)(2,1)} async-done(((bf16[3,2048,512]{1,2,0:T(8,128)(2,1)}), bf16[3,256,512]{1,2,0:T(8,128)(2,1)}) %reduce-scatter.21.cloned.1.call-update) | async-done | bytes 786448 | tf_op jit(solution)/shard_map/reduce_scatter | solution.py:304
  1681.5 148.1 %reduce-scatter.31.cloned.1.call-done = bf16[256,2048]{1,0:T(8,128)(2,1)} async-done(((bf16[2048,2048]{1,0:T(8,128)(2,1)}), bf16[256,2048]{1,0:T(8,128)(2,1)}) %reduce-scatter.31.cloned.1.call-update) | async-done | bytes 1048592 | tf_op jit(solution)/shard_map/reduce_scatter | solution.py:310
  1829.7 151.7 %reduce-scatter.29.cloned.1.call-done = bf16[256,2048]{1,0:T(8,128)(2,1)} async-done(((bf16[2048,2048]{1,0:T(8,128)(2,1)}), bf16[256,2048]{1,0:T(8,128)(2,1)}) %reduce-scatter.29.cloned.1.call-update) | async-done | bytes 1048592 | tf_op jit(solution)/shard_map/reduce_scatter | solution.py:310
  1985.2 148.5 %reduce-scatter.35.cloned.1.call-done = bf16[2048,256]{1,0:T(8,128)(2,1)} async-done(((bf16[2048,2048]{1,0:T(8,128)(2,1)}), bf16[2048,256]{1,0:T(8,128)(2,1)}) %reduce-scatter.35.cloned.1.call-update) | async-done | bytes 1048592 | tf_op jit(solution)/shard_map/reduce_scatter | solution.py:313
  2133.7 151.9 %reduce-scatter.33.cloned.1.call-done = bf16[2048,256]{1,0:T(8,128)(2,1)} async-done(((bf16[2048,2048]{1,0:T(8,128)(2,1)}), bf16[2048,256]{1,0:T(8,128)(2,1)}) %reduce-scatter.33.cloned.1.call-update) | async-done | bytes 1048592 | tf_op jit(solution)/shard_map/reduce_scatter | solution.py:313
  (464 shorter events, 528.7 us)
Async XLA Ops:
  7.2 106.5 %all-gather.29.cloned.1.call-start = ((), (), s32[]{:S(2)}) async-start(), calls=%async_computation.30 | async-start | bytes 7077888 | tf_op jit(solution)/shard_map/all_gather | solution.py:161
  11.0 130.9 %all-gather.23.cloned.1.call-start = ((), (), s32[]{:S(2)}) async-start(), calls=%async_computation.13 | async-start | bytes 1572864 | tf_op jit(solution)/shard_map/all_gather | solution.py:180
  124.4 168.5 %all-gather.33.cloned.1.call-start = ((), (), s32[]{:S(2)}) async-start(), calls=%async_computation.32 | async-start | bytes 9437184 | tf_op jit(solution)/shard_map/all_gather | solution.py:163
  127.6 291.4 %all-gather.35.cloned.1.call-start = ((), (), s32[]{:S(2)}) async-start(), calls=%async_computation.33 | async-start | bytes 9437184 | tf_op jit(solution)/shard_map/all_gather | solution.py:164
  130.8 339.4 %all-gather.31.cloned.1.call-start = ((), (), s32[]{:S(2)}) async-start(), calls=%async_computation.31 | async-start | bytes 2359296 | tf_op jit(solution)/shard_map/all_gather | solution.py:162
  132.7 392.7 %all-reduce.6.cloned.1.call-start = ((), (), s32[]{:S(2)}) async-start(), calls=%async_computation.14 | async-start | bytes 4194304 | tf_op jit(solution)/shard_map/psum | solution.py:196
  475.7 152.6 %all-gather.37.cloned.1.call-start = ((), (), s32[]{:S(2)}) async-start(), calls=%async_computation.34 | async-start | bytes 7077888 | tf_op jit(solution)/shard_map/all_gather | solution.py:161
  476.9 179.8 %all-gather.27.cloned.1.call-start = ((), (), s32[]{:S(2)}) async-start(), calls=%async_computation.16 | async-start | bytes 1572864 | tf_op jit(solution)/shard_map/all_gather | solution.py:180
  639.2 94.2 %all-gather.39.cloned.1.call-start = ((), (), s32[]{:S(2)}) async-start(), calls=%async_computation.35 | async-start | bytes 2359296 | tf_op jit(solution)/shard_map/all_gather | solution.py:162
  640.0 218.8 %all-gather.41.cloned.1.call-start = ((), (), s32[]{:S(2)}) async-start(), calls=%async_computation.36 | async-start | bytes 9437184 | tf_op jit(solution)/shard_map/all_gather | solution.py:163
  640.5 344.6 %all-gather.43.cloned.1.call-start = ((), (), s32[]{:S(2)}) async-start(), calls=%async_computation.37 | async-start | bytes 9437184 | tf_op jit(solution)/shard_map/all_gather | solution.py:164
  641.3 366.3 %reduce-scatter.13.cloned.1.call-start = ((), (), s32[]{:S(2)}) async-start(), calls=%async_computation.17 | async-start | bytes 1572864 | tf_op jit(solution)/shard_map/reduce_scatter | solution.py:270
  779.2 249.6 %reduce-scatter.15.cloned.1.call-start = ((), (), s32[]{:S(2)}) async-start(), calls=%async_computation.18 | async-start | bytes 1572864 | tf_op jit(solution)/shard_map/reduce_scatter | solution.py:273
  871.6 217.8 %all-reduce.8.cloned.1.call-start = ((), (), s32[]{:S(2)}) async-start(), calls=%async_computation.19 | async-start | bytes 4194304 | tf_op jit(solution)/shard_map/psum | solution.py:297
  1037.8 150.9 %reduce-scatter.17.cloned.1.call-start = ((), (), s32[]{:S(2)}) async-start(), calls=%async_computation.20 | async-start | bytes 1572864 | tf_op jit(solution)/shard_map/reduce_scatter | solution.py:270
  1165.9 125.3 %all-reduce.10.cloned.1.call-start = ((), (), s32[]{:S(2)}) async-start(), calls=%async_computation.38 | async-start | bytes 8388608 | tf_op jit(solution)/shard_map/psum | solution.py:196
  1205.2 158.3 %reduce-scatter.27.cloned.1.call-start = ((), (), s32[]{:S(2)}) async-start(), calls=%async_computation.25 | async-start | bytes 2359296 | tf_op jit(solution)/shard_map/reduce_scatter | solution.py:307
  1210.5 224.1 %reduce-scatter.25.cloned.1.call-start = ((), (), s32[]{:S(2)}) async-start(), calls=%async_computation.24 | async-start | bytes 2359296 | tf_op jit(solution)/shard_map/reduce_scatter | solution.py:307
  1215.1 340.9 %reduce-scatter.23.cloned.1.call-start = ((), (), s32[]{:S(2)}) async-start(), calls=%async_computation.23 | async-start | bytes 7077888 | tf_op jit(solution)/shard_map/reduce_scatter | solution.py:304
  1223.5 454.1 %reduce-scatter.21.cloned.1.call-start = ((), (), s32[]{:S(2)}) async-start(), calls=%async_computation.22 | async-start | bytes 7077888 | tf_op jit(solution)/shard_map/reduce_scatter | solution.py:304
  1231.6 598.1 %reduce-scatter.31.cloned.1.call-start = ((), (), s32[]{:S(2)}) async-start(), calls=%async_computation.27 | async-start | bytes 9437184 | tf_op jit(solution)/shard_map/reduce_scatter | solution.py:310
  1241.8 739.5 %reduce-scatter.29.cloned.1.call-start = ((), (), s32[]{:S(2)}) async-start(), calls=%async_computation.26 | async-start | bytes 9437184 | tf_op jit(solution)/shard_map/reduce_scatter | solution.py:310
  1251.0 882.7 %reduce-scatter.35.cloned.1.call-start = ((), (), s32[]{:S(2)}) async-start(), calls=%async_computation.29 | async-start | bytes 9437184 | tf_op jit(solution)/shard_map/reduce_scatter | solution.py:313
  1263.0 1022.6 %reduce-scatter.33.cloned.1.call-start = ((), (), s32[]{:S(2)}) async-start(), calls=%async_computation.28 | async-start | bytes 9437184 | tf_op jit(solution)/shard_map/reduce_scatter | solution.py:313
  (96 other events, 5686.0 us)
Sparse Core Ops, SparseCore 0:
  11.1 102.6 all-gather.28
  144.0 21.2 all-gather.20
  167.9 124.9 all-gather.32
  295.4 123.5 all-gather.34
  420.9 49.2 all-gather.30
  475.8 49.5 all-reduce.5
  528.2 99.9 all-gather.36
  658.8 21.2 all-gather.24
  682.3 51.0 all-gather.38
  735.7 123.0 all-gather.40
  861.6 123.5 all-gather.42
  1008.5 20.2 reduce-scatter.14
  1037.9 51.3 all-reduce.7
  1151.7 20.3 reduce-scatter.16
  1174.3 20.3 reduce-scatter.18
  1205.4 85.7 all-reduce.9
  1294.9 68.5 reduce-scatter.26
  1367.5 67.0 reduce-scatter.24
  1438.7 117.3 reduce-scatter.22
  1560.1 117.4 reduce-scatter.20
  1681.5 148.1 reduce-scatter.30
  1833.3 147.9 reduce-scatter.28
  1985.3 148.3 reduce-scatter.34
  2137.2 148.3 reduce-scatter.32
  (3 shorter events, 57.3 us)
where the time goes:
time: 2300 us
  waiting for transfers between devices  1770 us (77%)
  matrix products  314 us (14%)
  other arithmetic  95.3 us (4%)
  local copies, waits for them, and re-layouts  58 us (3%)
  blocking collectives  38.9 us (2%)
    reduce_scatter x2, waiting for transfers between devices, on_device(): lax.psum_scatter(grad_down_w.astype(jnp.bfloat16), ('slot', 'ctx'), scatt...  300 us
    reduce_scatter x2, waiting for transfers between devices, on_device(): lax.psum_scatter(grad_up_w.astype(jnp.bfloat16), ('slot', 'ctx'), scatter...  300 us
    reduce_scatter x2, waiting for transfers between devices, on_device(): lax.psum_scatter(grad_qkv_w.astype(jnp.bfloat16), ('slot', 'ctx'), scatte...  241 us
    all_gather x2, waiting for transfers between devices, on_device(): lax.all_gather(w_down[layer_idx], ('slot', 'ctx'), axis=1, tiled=True)  230 us
    all_gather x2, waiting for transfers between devices, on_device(): lax.all_gather(w_qkv[layer_idx], ('slot', 'ctx'), axis=1, tiled=True)  197 us
    all_gather x2, waiting for transfers between devices, on_device(): lax.all_gather(w_up[layer_idx], ('slot', 'ctx'), axis=0, tiled=True)  190 us
    reduce_scatter x2, waiting for transfers between devices, on_device(): lax.psum_scatter(grad_out_w.astype(jnp.bfloat16), ('slot', 'ctx'), scatte...  88.1 us
    all_gather x2, waiting for transfers between devices, on_device(): lax.all_gather(w_out[layer_idx], ('slot', 'ctx'), axis=1, tiled=True)  77.6 us
  transfers between devices with their start and end apart: 27, of which 22 were waited for; matrix products, arithmetic and copies ran while one was open for 15% of the time, Pallas kernels for 0%

commit v1 on v0

v1 whole, which is shorter than its diff:
```python
import functools
import math

import jax
import jax.numpy as jnp
from jax import lax
from jax.experimental import pallas as pl
from jax.experimental.pallas import tpu as pltpu
from jax.sharding import PartitionSpec as P

HD = 64
ROT = 32
LAYERS = 2

masked = -1e30
F32 = jnp.float32
BF16 = jnp.bfloat16
NT = (((1,), (1,)), ((), ()))
TN = (((0,), (0,)), ((), ()))
VMEM_LIMIT = 20 * 1024 * 1024


def dot(a, b, dims=None):
    if dims is None:
        return jnp.dot(a, b, preferred_element_type=F32)
    return lax.dot_general(a, b, dims, preferred_element_type=F32)


def gelu_tanh(value):
    inner = 0.7978845608028654 * (value + 0.044715 * value * value * value)
    return 0.5 * value * (1.0 + jnp.tanh(inner))


def gelu_slope(value):
    square = value * value
    inner = 0.7978845608028654 * (value + 0.044715 * value * square)
    bend = jnp.tanh(inner)
    slope = 0.7978845608028654 * (1.0 + 3.0 * 0.044715 * square)
    return 0.5 * (1.0 + bend) + 0.5 * value * (1.0 - bend * bend) * slope


def layer_norm(hidden, gain, shift):
    centre = jnp.mean(hidden, -1, keepdims=True)
    centred = hidden - centre
    variance = jnp.mean(centred * centred, -1, keepdims=True)
    return centred * lax.rsqrt(variance + 1e-05) * gain + shift


def rotary_tables(positions, heads):
    half_rot = ROT // 2
    freqs = jnp.exp(jnp.arange(half_rot, dtype=F32) * (-2.0 * math.log(10000.0) / ROT))
    angles = positions.astype(F32)[:, None] * freqs[None, :]
    cosine, sine = jnp.cos(angles), jnp.sin(angles)
    rows = positions.shape[0]
    rest = jnp.zeros((rows, HD - ROT), F32)
    none = jnp.zeros_like(sine)
    same = jnp.concatenate([cosine, cosine, rest + 1.0], axis=1)
    ahead = jnp.concatenate([-sine, none, rest], axis=1)
    behind = jnp.concatenate([none, sine, rest], axis=1)
    return jnp.stack([jnp.tile(part, (1, heads)) for part in (same, ahead, behind)])


def turn(value, tables, back=False):
    width = value.shape[1]
    half_rot = ROT // 2
    moved = (
        pltpu.roll(value, width - half_rot, 1) * tables[1] + pltpu.roll(value, half_rot, 1) * tables[2]
    )
    stay = value * tables[0]
    return stay - moved if back else stay + moved


def in_kernel(count, *refs):
    xs = refs[:count]
    w_ref, bias_ref, table_ref, q_ref, kv_ref, up_ref, act_ref = refs[count:]
    n = q_ref.shape[1]
    rows = xs[0].shape[0]
    half = count // 2
    for part in range(2):
        at = slice(part * half * rows, (part + 1) * half * rows)
        x = jnp.concatenate([ref[...] for ref in xs[part * half : (part + 1) * half]], axis=0)
        out = dot(x, w_ref[...]) + bias_ref[...]
        tables = table_ref[:, at]
        q_ref[at, :] = turn(out[:, :n], tables).astype(BF16)
        kv_ref[at, :n] = turn(out[:, n : 2 * n], tables).astype(BF16)
        kv_ref[at, n:] = out[:, 2 * n : 3 * n].astype(BF16)
        up = out[:, 3 * n :]
        up_ref[at, :] = up
        act_ref[at, :] = gelu_tanh(up).astype(BF16)


def rows_of(block, width):
    return pl.BlockSpec((block, width), lambda i: (i, 0))


def whole(*shape):
    return pl.BlockSpec(shape, lambda i: (0,) * len(shape))


def params():
    return pltpu.CompilerParams(
        dimension_semantics=("arbitrary",), vmem_limit_bytes=VMEM_LIMIT
    )


def plain():
    return pltpu.CompilerParams(vmem_limit_bytes=VMEM_LIMIT)


def cost(flops, moved=0):
    return pl.CostEstimate(
        flops=int(COST_SCALE * flops), bytes_accessed=int(moved), transcendentals=0
    )


COST_SCALE = 1.5
COST = cost(1000)


def in_project(xs, win, bias, tables, n):
    rows, width = xs[0].shape
    run = rows * len(xs)
    f = win.shape[1] - 3 * n
    shape = jax.ShapeDtypeStruct
    return pl.pallas_call(
        functools.partial(in_kernel, len(xs)),
        out_shape=[
            shape((run, n), BF16),
            shape((run, 2 * n), BF16),
            shape((run, f), F32),
            shape((run, f), BF16),
        ],
        compiler_params=plain(),
        cost_estimate=cost(2 * run * width * win.shape[1], 2 * win.size),
        name="in_project",
    )(*xs, win, bias, tables)


def diagonal(block, corner, rows_each, room):
    key = lax.broadcasted_iota(jnp.int32, (block, block), 0)
    query = lax.broadcasted_iota(jnp.int32, (1, block), 1)
    inside = corner % (block // rows_each)

    def at(row):
        return (row // rows_each ^ inside) * rows_each + row % rows_each

    return at(key) < jnp.minimum(at(query) + 1, room)


def attend_kernel(rows_each, at_ref, q_ref, own_ref, prev_ref, res_ref, att_ref, lse_ref):
    length, place, corner = at_ref[0], at_ref[1], at_ref[2]
    block, n = q_ref.shape
    heads = n // HD
    run = own_ref.shape[0]
    i = pl.program_id(0)
    flip = corner * rows_each // block
    home = i ^ flip
    first = place * run + home * block

    @pl.when(first >= length)
    def _():
        res_ref[...] = jnp.zeros_like(res_ref)
        att_ref[...] = jnp.zeros_like(att_ref)
        lse_ref[...] = jnp.zeros_like(lse_ref)

    @pl.when(first < length)
    def _():
        lane = lax.broadcasted_iota(jnp.int32, (1, n), 1)
        q = q_ref[...].astype(F32) * HD ** (-0.5)
        qs = [jnp.where(lane // HD == h, q, 0.0).astype(BF16) for h in range(heads)]

        def step(keys, values, carry, limit=None):
            out = []
            for h in range(heads):
                top, total, accum = carry[h]
                scores = dot(keys, qs[h], NT)
                if limit is not None:
                    scores = jnp.where(limit, scores, masked)
                new_top = jnp.maximum(top, jnp.max(scores, 0, keepdims=True))
                probs = jnp.exp(scores - new_top)
                shrink = jnp.exp(top - new_top)
                total = total * shrink + jnp.sum(probs, 0, keepdims=True)
                accum = accum * shrink + dot(values, probs.astype(BF16), TN)
                out.append((new_top, total, accum))
            return tuple(out)

        carry = tuple(
            (
                jnp.full((1, block), masked, F32),
                jnp.zeros((1, block), F32),
                jnp.zeros((n, block), F32),
            )
            for _ in range(heads)
        )
        inner = run // block

        def prev_step(j, carry):
            rows = pl.ds(pl.multiple_of((j % inner) * block, block), block)
            return step(prev_ref[j // inner, rows, :n], prev_ref[j // inner, rows, n:], carry)

        carry = lax.fori_loop(0, place * inner, prev_step, carry)

        def own_step(j, carry):
            rows = pl.ds(pl.multiple_of((j ^ flip) * block, block), block)
            return step(own_ref[rows, :n], own_ref[rows, n:], carry)

        carry = lax.fori_loop(0, home, own_step, carry)
        limit = diagonal(block, corner, rows_each, length - first)
        rows = pl.ds(pl.multiple_of(i * block, block), block)
        carry = step(own_ref[rows, :n], own_ref[rows, n:], carry, limit)
        parts = []
        for h in range(heads):
            top, total, accum = carry[h]
            lse_ref[h : h + 1, :] = top + jnp.log(total)
            parts.append(accum[h * HD : (h + 1) * HD] / total)
        result = jnp.concatenate(parts, axis=0).T
        res_ref[...] = result
        att_ref[...] = result.astype(BF16)


def attend(at, q, kv, prev, block, rows_each):
    run, n = q.shape
    heads = n // HD
    before = prev.shape[0]
    shape = jax.ShapeDtypeStruct
    tiles = run * (before * run + run)
    return pl.pallas_call(
        functools.partial(attend_kernel, rows_each),
        grid=(run // block,),
        in_specs=[
            pl.BlockSpec(memory_space=pltpu.SMEM),
            rows_of(block, n),
            whole(run, 2 * n),
            whole(before, run, 2 * n),
        ],
        out_specs=[
            rows_of(block, n),
            rows_of(block, n),
            pl.BlockSpec((heads, block), lambda i: (0, i)),
        ],
        out_shape=[shape((run, n), F32), shape((run, n), BF16), shape((heads, run), F32)],
        compiler_params=params(),
        cost_estimate=cost(32 * run * (before * run + run) * n),
        name="attend",
    )(at, q, kv, prev)


def out_kernel(att_ref, act_ref, w_ref, *y_refs):
    rows = y_refs[0].shape[0]
    half = len(y_refs) // 2
    for part in range(2):
        at = slice(part * half * rows, (part + 1) * half * rows)
        both = jnp.concatenate([att_ref[at, :], act_ref[at, :]], axis=1)
        out = dot(both, w_ref[...], NT).astype(BF16)
        for j in range(half):
            y_refs[part * half + j][...] = out[j * rows : (j + 1) * rows]


def out_project(att, act, wout, rows):
    count = att.shape[0] // rows
    return pl.pallas_call(
        out_kernel,
        out_shape=[jax.ShapeDtypeStruct((rows, wout.shape[0]), BF16)] * count,
        compiler_params=plain(),
        cost_estimate=cost(2 * att.shape[0] * wout.size, 2 * wout.size),
        name="out_project",
    )(att, act, wout)


def out_back_kernel(count, *refs):
    xs = refs[:count]
    w_ref, up_ref, gatt_ref, gup_ref = refs[count:]
    n = gatt_ref.shape[1]
    rows = xs[0].shape[0]
    half = count // 2
    for part in range(2):
        at = slice(part * half * rows, (part + 1) * half * rows)
        x = jnp.concatenate([ref[...] for ref in xs[part * half : (part + 1) * half]], axis=0)
        out = dot(x, w_ref[...])
        gatt_ref[at, :] = out[:, :n].astype(BF16)
        gup_ref[at, :] = (out[:, n:] * gelu_slope(up_ref[at, :])).astype(BF16)


def out_back(xs, wout, up, n):
    run, f = up.shape
    shape = jax.ShapeDtypeStruct
    return pl.pallas_call(
        functools.partial(out_back_kernel, len(xs)),
        out_shape=[shape((run, n), BF16), shape((run, f), BF16)],
        compiler_params=plain(),
        cost_estimate=cost(2 * run * wout.size, 2 * wout.size),
        name="out_back",
    )(*xs, wout, up)


def attend_back_kernel(
    rows_each, at_ref, q_ref, own_ref, prev_ref, gatt_ref, res_ref, lse_ref, table_ref,
    gq_ref, gown_ref, gprev_ref, hold_ref,
):
    length, place, corner = at_ref[0], at_ref[1], at_ref[2]
    block, n = q_ref.shape
    heads = n // HD
    run = own_ref.shape[0]
    before = prev_ref.shape[0]
    i = pl.program_id(0)
    flip = corner * rows_each // block
    home = i ^ flip
    first = place * run + home * block

    @pl.when(i == 0)
    def _():
        gown_ref[...] = jnp.zeros_like(gown_ref)
        hold_ref[...] = jnp.zeros_like(hold_ref)

    @pl.when(first >= length)
    def _():
        gq_ref[...] = jnp.zeros_like(gq_ref)

    @pl.when(first < length)
    def _():
        lane = lax.broadcasted_iota(jnp.int32, (1, n), 1)
        q, gatt = q_ref[...], gatt_ref[...]
        pick = [lane // HD == h for h in range(heads)]
        zero = jnp.zeros((), BF16)
        qs = [jnp.where(p, q, zero) for p in pick]
        gs = [jnp.where(p, gatt, zero) for p in pick]
        shared = (gatt.astype(F32) * res_ref[...]).T
        deltas = [jnp.sum(shared[h * HD : (h + 1) * HD], 0, keepdims=True) for h in range(heads)]
        sums = [lse_ref[h : h + 1, :] for h in range(heads)]
        scale = HD ** (-0.5)

        def step(keys, values, carry, limit=None):
            gkeys = gvalues = None
            out = []
            for h in range(heads):
                scores = dot(keys, qs[h], NT) * scale
                if limit is not None:
                    scores = jnp.where(limit, scores, masked)
                probs = jnp.exp(scores - sums[h])
                gprobs = dot(values, gs[h], NT)
                gscores = (probs * (gprobs - deltas[h]) * scale).astype(BF16)
                gvalue = dot(probs.astype(BF16), gs[h])
                gkey = dot(gscores, qs[h])
                gkeys = gkey if gkeys is None else gkeys + gkey
                gvalues = gvalue if gvalues is None else gvalues + gvalue
                out.append(carry[h] + dot(keys, gscores, TN))
            return tuple(out), gkeys, gvalues

        carry = tuple(jnp.zeros((n, block), F32) for _ in range(heads))
        inner = run // block

        def prev_step(j, carry):
            k, rows = j // inner, pl.ds(pl.multiple_of((j % inner) * block, block), block)
            carry, gkeys, gvalues = step(prev_ref[k, rows, :n], prev_ref[k, rows, n:], carry)
            hold_ref[k, rows, :n] += gkeys
            hold_ref[k, rows, n:] += gvalues
            return carry

        carry = lax.fori_loop(0, place * inner, prev_step, carry)

        def own_step(j, carry):
            rows = pl.ds(pl.multiple_of((j ^ flip) * block, block), block)
            carry, gkeys, gvalues = step(own_ref[rows, :n], own_ref[rows, n:], carry)
            gown_ref[rows, :n] += gkeys
            gown_ref[rows, n:] += gvalues
            return carry

        carry = lax.fori_loop(0, home, own_step, carry)
        limit = diagonal(block, corner, rows_each, length - first)
        rows = pl.ds(pl.multiple_of(i * block, block), block)
        carry, gkeys, gvalues = step(own_ref[rows, :n], own_ref[rows, n:], carry, limit)
        gown_ref[rows, :n] += gkeys
        gown_ref[rows, n:] += gvalues
        gq = jnp.concatenate([carry[h][h * HD : (h + 1) * HD] for h in range(heads)], axis=0).T
        gq_ref[...] = turn(gq, table_ref[...], back=True).astype(BF16)

    @pl.when(i == pl.num_programs(0) - 1)
    def _():
        gprev_ref[...] = hold_ref[...].astype(BF16)


def attend_back(at, q, kv, prev, gatt, res, lse, tables, block, rows_each):
    run, n = q.shape
    heads = n // HD
    before = prev.shape[0]
    shape = jax.ShapeDtypeStruct
    tiles = run * (before * run + run)
    return pl.pallas_call(
        functools.partial(attend_back_kernel, rows_each),
        grid=(run // block,),
        in_specs=[
            pl.BlockSpec(memory_space=pltpu.SMEM),
            rows_of(block, n),
            whole(run, 2 * n),
            whole(before, run, 2 * n),
            rows_of(block, n),
            rows_of(block, n),
            pl.BlockSpec((heads, block), lambda i: (0, i)),
            pl.BlockSpec((3, block, n), lambda i: (0, i, 0)),
        ],
        out_specs=[rows_of(block, n), whole(run, 2 * n), whole(before, run, 2 * n)],
        out_shape=[
            shape((run, n), BF16),
            shape((run, 2 * n), F32),
            shape((before, run, 2 * n), BF16),
        ],
        scratch_shapes=[pltpu.VMEM((before, run, 2 * n), F32)],
        compiler_params=params(),
        cost_estimate=cost(32 * run * (before * run + run) * n),
        name="attend_back",
    )(at, q, kv, prev, gatt, res, lse, tables)


def in_back_kernel(
    gq_ref, gkv_ref, got_ref, gup_ref, w_ref, table_ref, gin_ref, bias_ref, *y_refs
):
    n = gq_ref.shape[1]
    rows = y_refs[0].shape[0]
    half = len(y_refs) // 2
    sums = None
    for part in range(2):
        at = slice(part * half * rows, (part + 1) * half * rows)
        gkv = gkv_ref[at, :]
        for j in range(got_ref.shape[0]):
            gkv = gkv + got_ref[j, at, :].astype(F32)
        gkey = turn(gkv[:, :n], table_ref[:, at], back=True).astype(BF16)
        gin = jnp.concatenate(
            [gq_ref[at, :], gkey, gkv[:, n:].astype(BF16), gup_ref[at, :]], axis=1
        )
        gin_ref[at, :] = gin
        out = dot(gin, w_ref[...], NT).astype(BF16)
        for j in range(half):
            y_refs[part * half + j][...] = out[j * rows : (j + 1) * rows]
        term = jnp.sum(gin.astype(F32), 0, keepdims=True)
        sums = term if sums is None else sums + term
    bias_ref[...] = sums


def in_back(gq, gkv, got, gup, win, tables, rows):
    run = gq.shape[0]
    width, wide = win.shape
    shape = jax.ShapeDtypeStruct
    return pl.pallas_call(
        in_back_kernel,
        out_shape=[shape((run, wide), BF16), shape((1, wide), F32)]
        + [shape((rows, width), BF16)] * (run // rows),
        compiler_params=plain(),
        cost_estimate=cost(2 * run * width * wide, 2 * win.size),
        name="in_back",
    )(gq, gkv, got, gup, win, tables)


def weight_grad_kernel(count, slots, *refs):
    xs, ys, out_ref, hold_ref = refs[:count], refs[count:-2], refs[-2], refs[-1]

    @pl.when(pl.program_id(0) == 0)
    def _():
        col = 0
        for j in range(len(ys) // slots):
            for m in range(slots):
                y_ref = ys[j * slots + m]
                run, wide = y_ref.shape
                hold_ref[m * run : (m + 1) * run, col : col + wide] = y_ref[...]
            col += wide

    left = jnp.concatenate([ref[...] for ref in xs], axis=0)
    out_ref[...] = dot(left, hold_ref[...], TN).astype(BF16)


def weight_grad(xs, ys, block):
    rows, width = xs[0].shape
    tokens = rows * len(xs)
    slots = len(ys[0])
    wide = sum(part[0].shape[1] for part in ys)
    flat = [array for part in ys for array in part]
    return pl.pallas_call(
        functools.partial(weight_grad_kernel, len(xs), slots),
        grid=(width // block,),
        in_specs=[pl.BlockSpec((rows, block), lambda i: (0, i)) for _ in xs]
        + [whole(*array.shape) for array in flat],
        out_specs=rows_of(block, wide),
        out_shape=jax.ShapeDtypeStruct((width, wide), BF16),
        scratch_shapes=[pltpu.VMEM((tokens, wide), BF16)],
        compiler_params=params(),
        cost_estimate=cost(2 * tokens * width * wide, 2 * tokens * (width + wide)),
        name="weight_grad",
    )(*xs, *flat)


def at_part(index, size):
    return pl.ds(pl.multiple_of(index * size, size), size)


def pack_in_kernel(at_ref, qkv_ref, up_ref, *out_refs):
    count = len(out_refs)
    n, f = qkv_ref.shape[3] // count, up_ref.shape[2] // count
    for k, out_ref in enumerate(out_refs):
        place = (at_ref[0] + k) % count
        for j in range(3):
            out_ref[:, j * n : (j + 1) * n] = qkv_ref[0, j, :, at_part(place, n)]
        out_ref[:, 3 * n :] = up_ref[0, :, at_part(place, f)]


def pack_out_kernel(at_ref, out_w_ref, down_ref, *out_refs):
    count = len(out_refs)
    n, f = out_w_ref.shape[1] // count, down_ref.shape[1] // count
    for k, out_ref in enumerate(out_refs):
        place = (at_ref[0] + k) % count
        out_ref[:, :n] = out_w_ref[0, at_part(place, n), :].astype(F32).T.astype(BF16)
        out_ref[:, n:] = down_ref[0, at_part(place, f), :].astype(F32).T.astype(BF16)


def pack(kernel, at, first, second, layer, shape, count):
    def of_layer(array):
        rest = array.shape[1:]
        return pl.BlockSpec((1, *rest), lambda i: (layer,) + (0,) * len(rest))

    return pl.pallas_call(
        kernel,
        grid=(1,),
        in_specs=[pl.BlockSpec(memory_space=pltpu.SMEM), of_layer(first), of_layer(second)],
        out_specs=[whole(*shape)] * count,
        out_shape=[jax.ShapeDtypeStruct(shape, BF16)] * count,
        compiler_params=params(),
        cost_estimate=COST,
        name="pack",
    )(at, first, second)


def place_kernel(count, at_ref, *refs):
    blocks, out_ref, sems = refs[:count], refs[count], refs[count + 1]
    copies = [
        pltpu.make_async_copy(blocks[k], out_ref.at[at_ref[k]], sems.at[k]) for k in range(count)
    ]
    for copy in copies:
        copy.start()
    for copy in copies:
        copy.wait()


def place(places, blocks):
    count = len(blocks)
    return pl.pallas_call(
        functools.partial(place_kernel, count),
        in_specs=[pl.BlockSpec(memory_space=pltpu.SMEM)]
        + [pl.BlockSpec(memory_space=pltpu.VMEM)] * count,
        out_specs=pl.BlockSpec(memory_space=pl.ANY),
        out_shape=jax.ShapeDtypeStruct((count, *blocks[0].shape), BF16),
        scratch_shapes=[pltpu.SemaphoreType.DMA((count,))],
        compiler_params=plain(),
        cost_estimate=COST,
        name="place",
    )(jnp.stack(places), *blocks)


def unpack_in_kernel(held, at_ref, *refs):
    blocks, (qkv_ref, up_ref) = refs[: -2 - held], refs[-2:]
    count = len(blocks)
    n, f = qkv_ref.shape[3] // count, up_ref.shape[2] // count
    for k, block_ref in enumerate(blocks):
        source = (at_ref[0] + count - k) % count
        value = block_ref[...].astype(F32)
        for j in range(3):
            qkv_ref[0, j, :, at_part(source, n)] = value[:, j * n : (j + 1) * n]
        up_ref[0, :, at_part(source, f)] = value[:, 3 * n :]


def unpack_out_kernel(held, at_ref, *refs):
    blocks, (out_ref, down_ref) = refs[: -2 - held], refs[-2:]
    count = len(blocks)
    n, f = out_ref.shape[1] // count, down_ref.shape[1] // count
    for k, block_ref in enumerate(blocks):
        source = (at_ref[0] + count - k) % count
        value = block_ref[...].astype(F32)
        out_ref[0, at_part(source, n), :] = value[:, :n].T
        down_ref[0, at_part(source, f), :] = value[:, n:].T


def unpack(kernel, at, blocks, layer, shapes, held):
    def of_layer(shape):
        return pl.BlockSpec((1, *shape[1:]), lambda i: (layer,) + (0,) * (len(shape) - 1))

    held = held or []
    first = 1 + len(blocks)
    return pl.pallas_call(
        functools.partial(kernel, len(held)),
        grid=(1,),
        in_specs=[pl.BlockSpec(memory_space=pltpu.SMEM)]
        + [whole(*block.shape) for block in blocks]
        + [pl.BlockSpec(memory_space=pl.ANY) for _ in held],
        out_specs=[of_layer(shape) for shape in shapes],
        out_shape=[jax.ShapeDtypeStruct(shape, F32) for shape in shapes],
        input_output_aliases={first + j: j for j in range(len(held))},
        compiler_params=params(),
        cost_estimate=COST,
        name="unpack",
    )(at, *blocks, *held)


def norm_kernel(count, *refs):
    parts = refs[:count]
    hidden_ref, bias_ref, gain_ref, shift_ref, next_ref, normed_ref = refs[count:]
    hidden = hidden_ref[...] + bias_ref[...]
    for ref in parts:
        hidden = hidden + ref[...].astype(F32)
    next_ref[...] = hidden
    normed_ref[...] = layer_norm(hidden, gain_ref[...], shift_ref[...]).astype(BF16)


def sum_norm(parts, hidden, bias, gain, shift):
    shape = jax.ShapeDtypeStruct
    return pl.pallas_call(
        functools.partial(norm_kernel, len(parts)),
        out_shape=[shape(hidden.shape, F32), shape(hidden.shape, BF16)],
        compiler_params=plain(),
        cost_estimate=COST,
        name="sum_norm",
    )(*parts, hidden, bias[None], gain[None], shift[None])


def norm_back_kernel(count, *refs):
    parts = refs[:count]
    hidden_ref, grad_ref, gain_ref, next_ref, low_ref, ggain_ref, gshift_ref = refs[count:]
    total = parts[0][...].astype(F32)
    for ref in parts[1:]:
        total = total + ref[...].astype(F32)
    hidden = hidden_ref[...]
    centred = hidden - jnp.mean(hidden, -1, keepdims=True)
    factor = lax.rsqrt(jnp.mean(centred * centred, -1, keepdims=True) + 1e-05)
    xhat = centred * factor
    ggain_ref[...] = jnp.sum(total * xhat, 0, keepdims=True)
    gshift_ref[...] = jnp.sum(total, 0, keepdims=True)
    inner = total * gain_ref[...]
    first = jnp.mean(inner, -1, keepdims=True)
    second = jnp.mean(inner * xhat, -1, keepdims=True)
    grad = grad_ref[...] + factor * (inner - first - xhat * second)
    next_ref[...] = grad
    low_ref[...] = grad.astype(BF16)


def sum_norm_back(parts, hidden, grad, gain):
    shape = jax.ShapeDtypeStruct
    row = shape((1, hidden.shape[1]), F32)
    return pl.pallas_call(
        functools.partial(norm_back_kernel, len(parts)),
        out_shape=[shape(hidden.shape, F32), shape(hidden.shape, BF16), row, row],
        compiler_params=plain(),
        cost_estimate=COST,
        name="sum_norm_back",
    )(*parts, hidden, grad, gain[None])


class Stages:
    def __init__(self, token):
        self.token = token
        self.active = []
        self.count = 0

    def spawn(self, process):
        self.active.append((process, None))

    def hold(self, *arrays):
        return lax.optimization_barrier((self.token, *arrays))[1:]

    def step(self):
        self.count += 1
        given, moved = [], True
        while moved:
            moved, todo, self.active = False, self.active, []
            for process, value in todo:
                try:
                    out = process.send(value)
                except StopIteration:
                    moved = True
                    continue
                if out is WAIT:
                    self.active.append((process, None))
                else:
                    moved = True
                    given.append((process, out))
        flat, tree = jax.tree.flatten([out for _, out in given])
        flat = lax.optimization_barrier((self.token, *flat))
        self.token = flat[0]
        outs = jax.tree.unflatten(tree, flat[1:])
        self.active += [(process, out) for (process, _), out in zip(given, outs)]

    def run(self):
        while self.active:
            before = [id(process) for process, _ in self.active]
            self.step()
            assert self.count < 500


WAIT = object()


def until(ready):
    while not ready():
        yield WAIT


class Group:
    def __init__(self):
        self.S = lax.axis_size("slot")
        self.C = lax.axis_size("ctx")
        self.T = lax.axis_size("tp")
        self.s = lax.axis_index("slot")
        self.c = lax.axis_index("ctx")
        self.t = lax.axis_index("tp")
        assert self.S == 4 and self.T == 4
        self.far, self.near = self.T // 2, 1
        self.corner = (self.t % 2) * 2 + self.t // 2
        self.slot_at = self.s.astype(jnp.int32)[None]

    def swap(self, block, bit):
        return lax.ppermute(block, "tp", [(i, i ^ bit) for i in range(self.T)])

    def shift(self, block, k):
        S = self.S
        return lax.ppermute(block, "slot", [(i, (i + k) % S) for i in range(S)])

    def parts_of(self, array, rows):
        return [
            lax.dynamic_slice_in_dim(array, (self.corner ^ b) * rows, rows, 0)
            for b in range(self.T)
        ]

    def in_order(self, parts):
        rows = parts[0].shape[0]
        array = jnp.zeros((self.T * rows, *parts[0].shape[1:]), parts[0].dtype)
        for b, part in enumerate(parts):
            array = lax.dynamic_update_slice_in_dim(array, part, (self.corner ^ b) * rows, 0)
        return array

    def gather(self, block, own_parts, ready, sent=lambda: None):
        blocks = {0: block}
        if own_parts is not None:
            ready(0, own_parts)
        waiting = []
        order = [0, 1, 3, 2]
        for r in range(6):
            for k, parts in waiting:
                ready(k, parts + [self.swap(parts[1], self.near)])
            waiting = []
            if r == 5:
                return
            fresh = {}
            if r == 0:
                fresh[1] = self.shift(block, -1)
            elif r == 1:
                fresh[3] = self.shift(block, 1)
            elif r == 2:
                fresh["down"] = lax.ppermute(blocks[1], "slot", [(1, 0), (2, 1)])
                fresh["up"] = lax.ppermute(blocks[3], "slot", [(1, 2), (2, 3)])
            if r == 3:
                blocks[2] = lax.optimization_barrier(
                    jnp.where(self.s < 2, blocks["down"], blocks["up"])
                )
            if r < 4 and (r > 0 or own_parts is None):
                k = order[r]
                mine = blocks[k]
                parts = [mine, self.swap(mine, self.far), self.swap(mine, self.near)]
                fresh, parts = yield fresh, parts
                waiting = [(k, parts)]
            elif r < 4:
                (fresh,) = yield (fresh,)
            blocks.update(fresh)
            if r == 2:
                sent()

    def scatter(self, make, there, finish):
        order = [2, 1, 3, 0]
        near, far, from_two = {}, {}, {}
        got = []

        def total(k, *more):
            return lax.optimization_barrier(
                sum((a.astype(F32) for a in more), sum(a.astype(F32) for a in far[k])).astype(BF16)
            )

        for r in range(5):
            if r < 4:
                yield from until(lambda: there(order[r]))
            sent = {}
            if r >= 1:
                keep, give = near[order[r - 1]]
                away = (keep[1].astype(F32) + give[1].astype(F32)).astype(BF16)
                sent["far"] = (keep[0], give[0], self.swap(away, self.far))
            if r == 2:
                two = total(2)
                sent["up"] = lax.ppermute(two, "slot", [(0, 1), (1, 2)])
                sent["down"] = lax.ppermute(two, "slot", [(2, 1), (3, 2)])
            if r == 3:
                sent["got"] = self.shift(total(1, from_two["up"]), 1)
            if r == 4:
                sent["got"] = self.shift(total(3, from_two["down"]), -1)
            if r < 4:
                keep0, keep1, give0, give1 = make(order[r])
                sent["near"] = (
                    (keep0, keep1),
                    (self.swap(give0, self.near), self.swap(give1, self.near)),
                )
            sent, got = yield sent, got
            if "near" in sent:
                near[order[r]] = sent["near"]
            if "far" in sent:
                far[order[r - 1]] = sent["far"]
            if "up" in sent:
                from_two = sent
            if "got" in sent:
                got = got + [sent["got"]]
        finish(list(far[0]) + got)

    def ctx_before(self, block):
        C = self.C
        got = [
            lax.ppermute(block, "ctx", [(i, i + j) for i in range(C - j)])[None]
            for j in range(1, C)
        ]
        return got[0] if C == 2 else jnp.concatenate(got)

    def ctx_return(self, blocks):
        C = self.C
        got = [
            lax.ppermute(blocks[j - 1], "ctx", [(i, i - j) for i in range(j, C)])[None]
            for j in range(1, C)
        ]
        return got[0] if C == 2 else jnp.concatenate(got)

    def ctx_others(self, block):
        C = self.C
        return [
            lax.ppermute(block, "ctx", [(i, (i + j) % C) for i in range(C)]) for j in range(1, C)
        ]

    def gather_weights(self, pieces, done, sent):
        S, C = self.S, self.C
        d, wide = pieces[0].shape
        blocks, places = [pieces[0]], [0]
        others = []
        for shifts, back in (([1, 3], [0]), ([2], [1, 3]), ([], [2])):
            ready = dict(zip(places, blocks))
            got = [self.shift(pieces[k], k) for k in shifts]
            new = [self.ctx_others(ready[k]) for k in back]
            got, new, blocks, others, pieces = yield got, new, blocks, others, pieces
            blocks, places = blocks + got, places + shifts
            others = others + list(zip(back, new))
            if shifts == [2]:
                sent()
        flat, at = [], []
        for k, block in zip(places, blocks):
            flat.append(block)
            at.append(self.c * S + (self.s - k) % S)
        for k, found in others:
            for j, block in enumerate(found):
                flat.append(block)
                at.append((self.c - j - 1) % C * S + (self.s - k) % S)
        done(place(at, flat).reshape(C * S * d, wide))

    def gather_weights_later(self, pieces, done, sent, steps):
        S, C = self.S, self.C
        d, wide = pieces[0].shape
        first, pieces = yield [self.shift(pieces[1], 1)], pieces
        more, first, pieces = yield [self.shift(pieces[3], 3)], first, pieces
        first = first + more
        second, first, pieces = yield [self.shift(pieces[2], 2)], first, pieces
        sent()
        flat = place(
            [(self.s - k) % S for k in (0, 1, 3, 2)], [pieces[0], first[0], first[1], second[0]]
        )
        array = lax.all_gather(flat, "ctx")
        for _ in range(steps):
            yield ()
        done(array.reshape(C * S * d, wide))

    def scatter_weights(self, grad, done, steps):
        S, C = self.S, self.C
        wide = grad.shape[1]
        d = grad.shape[0] // (S * C)
        own = lax.psum_scatter(grad.reshape(C, S, d, wide), "ctx")
        for _ in range(steps):
            yield ()
        pieces = [
            lax.dynamic_index_in_dim(own, (self.s + k) % S, 0, keepdims=False) for k in range(S)
        ]
        first, pieces = yield [self.shift(pieces[1], 1)], pieces
        more, first, pieces = yield [self.shift(pieces[3], 3)], first, pieces
        first = first + more
        second, first, pieces = yield [self.shift(pieces[2], 2)], first, pieces
        done([pieces[0], first[0], second[0], first[1]])

    def add_up(self, small, part, finish):
        cut = small.shape[0]
        both = jnp.concatenate([small, part])
        for axis, size in (("slot", self.S), ("ctx", self.C)):
            bit = 1
            while bit < size:
                got = lax.ppermute(both, axis, [(i, i ^ bit) for i in range(size)])
                got, both = yield got, both
                both = both + got
                bit *= 2
        small, part = both[:cut], both[cut:]
        for bit in (self.far, self.near):
            got = self.swap(small, bit)
            got, small, part = yield got, small, part
            small = small + got
        finish(small, part)


def on_device(
    inputs,
    lengths,
    ln_gain,
    ln_shift,
    w_qkv,
    b_qkv,
    w_out,
    b_out,
    w_up,
    b_up,
    w_down,
    b_down,
    cotangent,
):
    grp = Group()
    S, C, T = grp.S, grp.C, grp.T
    _, run, width = inputs.shape
    rows = run // T
    nt, ft = w_qkv.shape[3], w_up.shape[2]
    n, f = nt // S, ft // S
    d = w_up.shape[1]
    block = run // 2
    stages = Stages(lengths)

    def to_held(array):
        lead = array.shape[:-1]
        return array.reshape(*lead, S, C, d).swapaxes(-3, -2).reshape(*lead, width)

    def from_held(array):
        lead = array.shape[:-1]
        return array.reshape(*lead, C, S, d).swapaxes(-3, -2).reshape(*lead, width)

    inputs, cotangent = to_held(inputs), to_held(cotangent)
    ln_gain, ln_shift = to_held(ln_gain), to_held(ln_shift)
    b_out, b_down = to_held(b_out), to_held(b_down)
    local = jnp.arange(run, dtype=jnp.int32)
    positions = grp.c * run + (local // rows ^ grp.corner) * rows + local % rows
    tables = rotary_tables(positions, n // HD)
    valid = (positions < lengths[0]).astype(F32)[:, None]
    own_valid = valid[:rows]
    box = {}
    kept = [[None] * S for _ in range(LAYERS)]
    normed = [[None] * S for _ in range(LAYERS)]
    grad_branch = [[None] * S for _ in range(LAYERS)]
    middle = [[None] * S for _ in range(LAYERS)]
    gins = [[None] * S for _ in range(LAYERS)]
    bias_sums = [[None] * S for _ in range(LAYERS)]
    small_sums = [None] * LAYERS

    def bias_part(bias, size):
        return lax.dynamic_slice_in_dim(bias, grp.s * size, size, bias.ndim - 1)

    biases = [
        jnp.concatenate([bias_part(b_qkv[layer], n).reshape(-1), bias_part(b_up[layer], f)])[None]
        for layer in range(LAYERS)
    ]
    def after(*keys):
        return until(lambda: all(key in box for key in keys))

    def mark(*key):
        return lambda *value: box.__setitem__(key, value[0] if value else True)

    def lengths_of_all():
        got = yield [grp.shift(lengths, -k) for k in range(1, S)]
        for k, value in enumerate([lengths] + list(got)):
            box["at", k] = jnp.concatenate([value, grp.c[None], grp.corner[None]])

    def in_weights(layer, *keys, later=None):
        yield from after(*keys)
        pieces = pack(
            pack_in_kernel, grp.slot_at, w_qkv, w_up, layer, (d, 3 * n + f), S
        )
        pieces = list(stages.hold(*pieces))
        if later is None:
            yield from grp.gather_weights(pieces, mark("win", layer), mark("win sent", layer))
        else:
            yield from grp.gather_weights_later(
                pieces, mark("win", layer), mark("win sent", layer), later
            )

    def out_weights(layer, *keys, later=None):
        yield from after(*keys)
        pieces = pack(pack_out_kernel, grp.slot_at, w_out, w_down, layer, (d, n + f), S)
        pieces = list(stages.hold(*pieces))
        if later is None:
            yield from grp.gather_weights(pieces, mark("wout", layer), mark("wout sent", layer))
        else:
            yield from grp.gather_weights_later(
                pieces, mark("wout", layer), mark("wout sent", layer), later
            )

    def forward_slot(layer, k, parts):
        yield from after(("win", layer), ("at", k))
        normed[layer][k] = parts
        q, kv, up, act = in_project(parts, box["win", layer], biases[layer], tables, n)
        if k == 2:
            prev = grp.ctx_before(kv)
            q, kv, up, act = yield q, kv, up, act
        else:
            q, kv, up, act = yield q, kv, up, act
            q, kv, up, act, prev = yield q, kv, up, act, grp.ctx_before(kv)
        res, att, lse = attend(box["at", k], q, kv, prev, block, rows)
        box["attended", layer, k] = True
        kept[layer][k] = (q, kv, prev, up, act, res, att, lse)

    def make_forward(layer):
        def make(k):
            return out_project(kept[layer][k][6], kept[layer][k][4], box["wout", layer], rows)

        return make

    def there_forward(layer):
        return lambda k: ("attended", layer, k) in box and ("wout", layer) in box

    def backward_slot(layer, k, parts):
        yield from after(("wout", layer), ("attended", layer, k))
        grad_branch[layer][k] = parts
        if all(grad_branch[layer]):
            box["grad gathered", layer] = True
        q, kv, prev, up, _, res, _, lse = kept[layer][k]
        gatt, gup = out_back(parts, box["wout", layer], up, n)
        gq, gkv, gprev = attend_back(
            box["at", k], q, kv, prev, gatt, res, lse, tables, block, rows
        )
        if k == 2:
            got = grp.ctx_return(gprev)
            gq, gkv, gup = yield gq, gkv, gup
        else:
            gq, gkv, gup, gprev = yield gq, gkv, gup, gprev
            gq, gkv, gup, got = yield gq, gkv, gup, grp.ctx_return(gprev)
        middle[layer][k] = (gq, gkv, got, gup)
        box["middle", layer, k] = True

    def make_backward(layer):
        def make(k):
            gq, gkv, got, gup = middle[layer][k]
            gin, bias_sum, *parts = in_back(gq, gkv, got, gup, box["win", layer], tables, rows)
            gins[layer][k] = gin
            bias_sums[layer][k] = bias_sum[0]
            box["gin", layer, k] = True
            return parts

        return make

    def there_backward(layer):
        return lambda k: ("middle", layer, k) in box

    def slot_ready(kind, layer):
        return lambda m, parts: stages.spawn(kind(layer, m, parts))

    def out_grads(layer, *keys, steps=4):
        yield from after(*keys)
        grad = weight_grad(
            [part for parts in grad_branch[layer] for part in parts],
            [[kept[layer][k][6] for k in range(S)], [kept[layer][k][4] for k in range(S)]],
            block,
        )
        (grad,) = yield (grad,)
        yield from grp.scatter_weights(grad, mark("grad out", layer), steps)

    def in_grads(layer, *keys, steps=4):
        yield from after(*keys, *[("gin", layer, k) for k in range(S)])
        grad = weight_grad(
            [part for parts in normed[layer] for part in parts], [gins[layer]], block
        )
        (grad,) = yield (grad,)
        yield from grp.scatter_weights(grad, mark("grad in", layer), steps)

    def first_gather(*keys):
        yield from after(*keys)
        own_rows = grp.parts_of(inputs[0], rows)
        parts = [
            layer_norm(part.astype(F32), ln_gain[0], ln_shift[0]).astype(BF16) for part in own_rows
        ]
        box["hidden", 0] = own_rows[0].astype(F32)
        parts = list(stages.hold(*parts))
        yield from grp.gather(
            parts[0], parts, slot_ready(forward_slot, 0), mark("normed sent", 0)
        )

    def next_gather(layer):
        yield from after(("hidden", layer))
        yield from grp.gather(
            box["normed", layer], None, slot_ready(forward_slot, layer), mark("normed sent", layer)
        )

    def forward_sum(layer, *keys):
        yield from after(*keys)

        def finish(parts):
            later = min(layer + 1, LAYERS - 1)
            box["hidden", layer + 1], box["normed", layer + 1] = sum_norm(
                parts,
                box["hidden", layer],
                b_out[layer] + b_down[layer],
                ln_gain[later],
                ln_shift[later],
            )

        yield from grp.scatter(make_forward(layer), there_forward(layer), finish)

    def last_gradient(*keys):
        yield from after(*keys)
        parts = [
            part.astype(F32) * valid[b * rows : (b + 1) * rows]
            for b, part in enumerate(grp.parts_of(cotangent[0], rows))
        ]
        box["grad", LAYERS] = parts[0]
        parts = list(stages.hold(*[part.astype(BF16) for part in parts]))
        yield from grp.gather(
            parts[0], parts, slot_ready(backward_slot, LAYERS - 1), mark("grad sent", LAYERS)
        )

    def next_gradient(layer):
        yield from after(("grad", layer))
        yield from grp.gather(
            box["grad low", layer],
            None,
            slot_ready(backward_slot, layer - 1),
            mark("grad sent", layer),
        )

    def backward_sum(layer):
        def finish(parts):
            grad_bias_out = jnp.sum(box["grad", layer + 1], 0)
            box["grad", layer], box["grad low", layer], grad_gain, grad_shift = sum_norm_back(
                parts, box["hidden", layer], box["grad", layer + 1], ln_gain[layer]
            )
            small_sums[layer] = (grad_gain[0], grad_shift[0], grad_bias_out)

        yield from grp.scatter(make_backward(layer), there_backward(layer), finish)

    def all_sums(*keys):
        yield from after(*keys)
        spread = []
        for layer in range(LAYERS):
            total = sum(bias_sums[layer][1:], bias_sums[layer][0])
            pieces = jnp.zeros((3 * nt + ft,), F32)
            for i in range(3):
                pieces = lax.dynamic_update_slice_in_dim(
                    pieces, total[i * n : (i + 1) * n], i * nt + grp.s * n, 0
                )
            spread.append(
                lax.dynamic_update_slice_in_dim(pieces, total[3 * n :], 3 * nt + grp.s * f, 0)
            )
        yield from grp.add_up(
            jnp.concatenate([piece for entry in small_sums for piece in entry]),
            jnp.concatenate(spread),
            lambda small, part: box.__setitem__("sums", (small, part)),
        )

    def all_rows(key, value, name):
        yield from after(key)
        block = from_held(value())
        parts = [block, grp.swap(block, grp.far), grp.swap(block, grp.near)]
        parts = yield parts
        box[name] = grp.in_order(list(parts) + [grp.swap(parts[1], grp.near)])[None]

    def all_grads(layer, *keys):
        yield from after(("grad in", layer), ("grad out", layer), *keys)
        box["final in", layer] = unpack(
            unpack_in_kernel,
            grp.slot_at,
            box["grad in", layer],
            layer,
            ((LAYERS, 3, d, nt), (LAYERS, d, ft)),
            box.get(("final in", layer + 1)),
        )
        box["final out", layer] = unpack(
            unpack_out_kernel,
            grp.slot_at,
            box["grad out", layer],
            layer,
            ((LAYERS, nt, d), (LAYERS, ft, d)),
            box.get(("final out", layer + 1)),
        )

    last = LAYERS - 1
    stages.spawn(in_weights(0))
    stages.spawn(lengths_of_all())
    stages.spawn(first_gather(("win sent", 0)))
    stages.spawn(forward_sum(0))
    stages.spawn(out_weights(0, ("normed sent", 0)))
    for layer in range(1, LAYERS):
        stages.spawn(in_weights(layer, ("wout", layer - 1), later=3))
        stages.spawn(next_gather(layer))
        if layer < last:
            stages.spawn(forward_sum(layer))
        stages.spawn(out_weights(layer, ("win sent", layer), later=3))
    stages.spawn(last_gradient(("normed sent", last)))
    for layer in reversed(range(LAYERS)):
        stages.spawn(backward_sum(layer))
        if layer > 0:
            stages.spawn(next_gradient(layer))
    stages.spawn(forward_sum(last, ("grad sent", last)))
    for layer in reversed(range(LAYERS)):
        stages.spawn(out_grads(layer, ("grad gathered", layer)))
        stages.spawn(in_grads(layer))
        stages.spawn(all_grads(layer, *([] if layer == last else [("final in", layer + 1)])))
    stages.spawn(
        all_rows(
            ("hidden", LAYERS), lambda: (box["hidden", LAYERS] * own_valid).astype(BF16), "block out"
        )
    )
    stages.spawn(all_rows(("grad", 0), lambda: box["grad low", 0], "grad input"))
    stages.spawn(all_sums(("grad", 0)))
    stages.run()

    small, part = box["sums"]
    small = from_held(small.reshape(LAYERS, 3, width))
    part = part.reshape(LAYERS, 3 * nt + ft)
    grad_qkv, grad_up = box["final in", 0]
    grad_out, grad_down = box["final out", 0]
    return (
        box["block out"],
        box["grad input"],
        small[:, 0],
        small[:, 1],
        grad_qkv,
        part[:, : 3 * nt].reshape(LAYERS, 3, nt),
        grad_out,
        small[:, 2],
        grad_up,
        part[:, 3 * nt :],
        grad_down,
        small[:, 2],
    )


def solution(mesh):
    return jax.shard_map(
        on_device,
        mesh=mesh,
        in_specs=(
            P("slot", "ctx", None),
            P("slot"),
            P(),
            P(),
            P(None, None, ("slot", "ctx"), "tp"),
            P(None, None, "tp"),
            P(None, "tp", ("slot", "ctx")),
            P(),
            P(None, ("slot", "ctx"), "tp"),
            P(None, "tp"),
            P(None, "tp", ("slot", "ctx")),
            P(),
            P("slot", "ctx", None),
        ),
        out_specs=(
            P("slot", "ctx", None),
            P("slot", "ctx", None),
            P(),
            P(),
            P(None, None, ("slot", "ctx"), "tp"),
            P(None, None, "tp"),
            P(None, "tp", ("slot", "ctx")),
            P(),
            P(None, ("slot", "ctx"), "tp"),
            P(None, "tp"),
            P(None, "tp", ("slot", "ctx")),
            P(),
        ),
        check_vma=False,
    )
```

time: 2300 us -> 1040 us (0.45)
  waiting for transfers between devices: 1770 us -> 334 us
  matrix products: 314 us -> 0 us
  Pallas kernels: 0 us -> 217 us
  starting transfers between devices: 2.08 us -> 208 us
  local copies, waits for them, and re-layouts: 58 us -> 206 us
  other arithmetic: 95.3 us -> 50.4 us
  blocking collectives: 38.9 us -> 0 us
    reduce_scatter x12 -> x4, waiting for transfers between devices: 948 us -> 0.01 us  [scatter_weights(): own = lax.psum_scatter(grad.reshape(C, S, d, wide), 'ctx')]
    all_gather x12 -> x2, waiting for transfers between devices: 712 us -> 0.02 us  [gather_weights_later(): array = lax.all_gather(flat, 'ctx')]
    ppermute x0 -> x184, waiting for transfers between devices: none -> 333 us  [the longest x43 211 us: shift(): return lax.ppermute(block, 'slot', [(i, (i + k) % S) for i in range(S)])]
    dot_general x52 -> x0, matrix products: 314 us -> none  [the longest x8 30.9 us: block_scores(): jnp.einsum('qhd,khd->hqk', query, key_block, preferred_element_type=jnp.f...]
    pallas_call x0 -> x68, Pallas kernels: none -> 217 us  [the longest x4 46.6 us: weight_grad(): pl.pallas_call(functools.partial(weight_grad_kernel, len(xs), slots), gri...]
    ppermute x0 -> x184, starting transfers between devices: none -> 208 us  [the longest x43 71.4 us: shift(): return lax.ppermute(block, 'slot', [(i, (i + k) % S) for i in range(S)])]
    unnamed x163 -> x860, local copies, waits for them, and re-layouts: 19.1 us -> 140 us
    psum x3 -> x0, waiting for transfers between devices: 109 us -> none  [the longest x2 57.1 us: on_device(): lax.psum(partial_sum.astype(jnp.bfloat16), 'tp').astype(jnp.float32)]
  transfers between devices with their start and end apart: 27 -> 190, of which waited for: 22 -> 46; matrix products, arithmetic and copies ran while one was open for 15% -> 11% of each run, Pallas kernels for 0% -> 20%
where the time goes in v1:
time: 1040 us; the launch traced here: 1030 us
  waiting for transfers between devices  334 us (32%)
  Pallas kernels  217 us (21%)
  starting transfers between devices  208 us (20%)
  local copies, waits for them, and re-layouts  206 us (20%)
  other arithmetic  50.4 us (5%)
  between operations  19.9 us (2%)
    ppermute x43, waiting for transfers between devices, shift(): return lax.ppermute(block, 'slot', [(i, (i + k) % S) for i in range(S)])  211 us
    unnamed x860, local copies, waits for them, and re-layouts  140 us
    ppermute x43, starting transfers between devices, shift(): return lax.ppermute(block, 'slot', [(i, (i + k) % S) for i in range(S)])  71.4 us
    pallas_call x4, Pallas kernels, weight_grad(): pl.pallas_call(functools.partial(weight_grad_kernel, len(xs), slots), gri...  46.6 us
    ppermute x98, starting transfers between devices, swap(): return lax.ppermute(block, 'tp', [(i, i ^ bit) for i in range(self.T)])  44.8 us
    pallas_call x8, Pallas kernels, in_project(): pl.pallas_call(functools.partial(in_kernel, len(xs)), out_shape=[shape((r...  29.4 us
    ppermute x8, starting transfers between devices, ctx_before(): lax.ppermute(block, 'ctx', [(i, i + j) for i in range(C - j)])[None]  29.1 us
    ppermute x8, waiting for transfers between devices, ctx_return(): lax.ppermute(blocks[j - 1], 'ctx', [(i, i - j) for i in range(j, C)])[None]  27.6 us
  transfers between devices with their start and end apart: 190, of which 46 were waited for; matrix products, arithmetic and copies ran while one was open for 11% of the time, Pallas kernels for 20%

profile of v1, /device:TPU:0, one launch (start us, length us, event | category | flops | bytes accessed | tf_op | source)
XLA Modules:
  0.0 1034.9 jit_solution(6218143565198549854)
XLA Ops:
  51.0 13.7 %collective-permute-done.6.refs_3_ = bf16[256,896]{1,0:T(8,128)(2,1)} collective-permute-done((bf16[256,896]{1,0:T(8,128)(2,1)}, bf16[256,896]{1,0:T(8,128)(2,1)}, u32[]{:S(2)}, u32[]{:S(2)}) %collective-permute-start.6) | collective-permute-done | bytes 458784 | tf_op jit(solution)/shard_map/ppermute | solution.py:720
  69.7 9.2 collective-permute-done.9.refs_7_
  78.9 13.4 %collective-permute-done.10.refs_0_.refs_4_ = bf16[128,2048]{1,0:T(8,128)(2,1)} collective-permute-done((bf16[128,2048]{1,0:T(8,128)(2,1)}, bf16[128,2048]{1,0:T(8,128)(2,1)}, u32[]{:S(2)}, u32[]{:S(2)}) %collective-permute-start.10) | collective-permute-done | bytes 524320 | tf_op jit(solution)/shard_map/ppermute | solution.py:720
  171.9 7.7 collective-permute-done.30
  249.1 18.3 %collective-permute-done.46.refs_3_ = bf16[256,896]{1,0:T(8,128)(2,1)S(1)} collective-permute-done((bf16[256,896]{1,0:T(8,128)(2,1)S(1)}, bf16[256,896]{1,0:T(8,128)(2,1)S(1)}, u32[]{:S(2)}, u32[]{:S(2)}) %collective-permute-start.46) | collective-permute-done | bytes 458784 | tf_op jit(solution)/shard_map/ppermute | solution.py:720
  281.2 20.4 %collective-permute-done.51.refs_1_ = bf16[256,640]{1,0:T(8,128)(2,1)S(1)} collective-permute-done((bf16[256,640]{1,0:T(8,128)(2,1)}, bf16[256,640]{1,0:T(8,128)(2,1)S(1)}, u32[]{:S(2)}, u32[]{:S(2)}) %collective-permute-start.51) | collective-permute-done | bytes 327712 | tf_op jit(solution)/shard_map/ppermute | solution.py:720
  310.3 17.4 %collective-permute-done.54.refs_2_ = bf16[256,640]{1,0:T(8,128)(2,1)S(1)} collective-permute-done((bf16[256,640]{1,0:T(8,128)(2,1)}, bf16[256,640]{1,0:T(8,128)(2,1)S(1)}, u32[]{:S(2)}, u32[]{:S(2)}) %collective-permute-start.54) | collective-permute-done | bytes 327712 | tf_op jit(solution)/shard_map/ppermute | solution.py:720
  336.9 21.1 %collective-permute-done.55.refs_3_ = bf16[256,640]{1,0:T(8,128)(2,1)S(1)} collective-permute-done((bf16[256,640]{1,0:T(8,128)(2,1)S(1)}, bf16[256,640]{1,0:T(8,128)(2,1)S(1)}, u32[]{:S(2)}, u32[]{:S(2)}) %collective-permute-start.55) | collective-permute-done | bytes 327712 | tf_op jit(solution)/shard_map/ppermute | solution.py:720
  401.0 7.4 collective-permute-done.67
  470.5 8.0 collective-permute-done.79
  512.3 10.6 %weight_grad.4 = bf16[2048,640]{1,0:T(8,128)(2,1)S(1)} custom-call(bf16[128,2048]{1,0:T(8,128)(2,1)} %get-tuple-element.983.refs_0_, bf16[128,2048]{1,0:T(8,128)(2,1)S(1)} %copy-done.44, bf16[128,2048]{1,0:T(8,128)(2,1)S(1)} %copy-done.42, bf16[128,2048]{1,0:T(8,128)(2,1)S(1)} %copy-done.40, bf16[128,2048]{1,0:T(8,128)(2,1)} %collective-permute-done.72.refs_0_.refs_4_, ...), custom_call_target="tpu_custom_call" | custom-call | flops 8053063680 | bytes 11010048 | tf_op jit(solution)/shard_map/weight_grad/pallas_call | solution.py:476
  544.7 10.5 %collective-permute-done.95 = bf16[128,2048]{1,0:T(8,128)(2,1)S(1)} collective-permute-done((bf16[128,2048]{1,0:T(8,128)(2,1)S(1)}, bf16[128,2048]{1,0:T(8,128)(2,1)S(1)}, u32[]{:S(2)}, u32[]{:S(2)}) %collective-permute-start.95) | collective-permute-done | bytes 524320 | tf_op jit(solution)/shard_map/ppermute | solution.py:716
  556.7 9.1 collective-permute-start.102
  579.8 12.7 %weight_grad.5 = bf16[2048,896]{1,0:T(8,128)(2,1)S(1)} custom-call(bf16[128,2048]{1,0:T(8,128)(2,1)} %get-tuple-element.952.refs_0_, bf16[128,2048]{1,0:T(8,128)(2,1)S(1)} %copy-done.162, bf16[128,2048]{1,0:T(8,128)(2,1)S(1)} %copy-done.165, bf16[128,2048]{1,0:T(8,128)(2,1)} %collective-permute-done.62.refs_3_, ...), custom_call_target="tpu_custom_call" | custom-call | flops 11274289152 | bytes 12058624 | tf_op jit(solution)/shard_map/weight_grad/pallas_call | solution.py:476
  633.1 17.5 %collective-permute-done.111.refs_3_ = bf16[256,640]{1,0:T(8,128)(2,1)S(1)} collective-permute-done((bf16[256,640]{1,0:T(8,128)(2,1)S(1)}, bf16[256,640]{1,0:T(8,128)(2,1)S(1)}, u32[]{:S(2)}, u32[]{:S(2)}) %collective-permute-start.111) | collective-permute-done | bytes 327712 | tf_op jit(solution)/shard_map/ppermute | solution.py:720
  668.6 13.7 %collective-permute-done.116.refs_2_ = bf16[256,640]{1,0:T(8,128)(2,1)S(1)} collective-permute-done((bf16[256,640]{1,0:T(8,128)(2,1)S(1)}, bf16[256,640]{1,0:T(8,128)(2,1)S(1)}, u32[]{:S(2)}, u32[]{:S(2)}) %collective-permute-start.116) | collective-permute-done | bytes 327712 | tf_op jit(solution)/shard_map/ppermute | solution.py:720
  743.9 10.7 %weight_grad.6 = bf16[2048,640]{1,0:T(8,128)(2,1)S(1)} custom-call(bf16[128,2048]{1,0:T(8,128)(2,1)S(1)} %copy-done.178, bf16[128,2048]{1,0:T(8,128)(2,1)S(1)} %copy-done.182, bf16[128,2048]{1,0:T(8,128)(2,1)S(1)} %copy-done.184, bf16[128,2048]{1,0:T(8,128)(2,1)S(1)} %copy-done.186, bf16[128,2048]{1,0:T(8,128)(2,1)S(1)} %copy-done.180, ...), custom_call_target="tpu_custom_call" | custom-call | flops 8053063680 | bytes 11010048 | tf_op jit(solution)/shard_map/weight_grad/pallas_call | solution.py:476
  768.5 10.3 collective-permute-done.144
  876.3 12.7 %weight_grad.7 = bf16[2048,896]{1,0:T(8,128)(2,1)S(1)} custom-call(bf16[128,2048]{1,0:T(8,128)(2,1)} %get-tuple-element.747.refs_0_, bf16[128,2048]{1,0:T(8,128)(2,1)S(1)} %copy-done.34, bf16[128,2048]{1,0:T(8,128)(2,1)S(1)} %copy-done.36, bf16[128,2048]{1,0:T(8,128)(2,1)S(1)} %copy-done.32, bf16[128,2048]{1,0:T(8,128)(2,1)} %collective-permute-done.10.refs_0_.refs_4_, ...), custom_call_target="tpu_custom_call" | custom-call | flops 11274289152 | bytes 12058624 | tf_op jit(solution)/shard_map/weight_grad/pallas_call | solution.py:476
  922.7 8.0 collective-permute-done.168.refs_1_
  942.4 8.8 collective-permute-done.174
  956.3 15.7 %collective-permute-done.178 = f32[19456]{0:T(1024)S(1)} collective-permute-done((f32[19456]{0:T(1024)S(1)}, f32[19456]{0:T(1024)S(1)}, u32[]{:S(2)}, u32[]{:S(2)}) %collective-permute-start.178) | collective-permute-done | bytes 77856 | tf_op jit(solution)/shard_map/ppermute | solution.py:898
  982.9 11.0 %collective-permute-done.176.refs_1_ = bf16[256,896]{1,0:T(8,128)(2,1)S(1)} collective-permute-done((bf16[256,896]{1,0:T(8,128)(2,1)S(1)}, bf16[256,896]{1,0:T(8,128)(2,1)S(1)}, u32[]{:S(2)}, u32[]{:S(2)}) %collective-permute-start.176) | collective-permute-done | bytes 458784 | tf_op jit(solution)/shard_map/ppermute | solution.py:720
  1009.1 15.7 %collective-permute-done.183.refs_2_ = bf16[256,896]{1,0:T(8,128)(2,1)S(1)} collective-permute-done((bf16[256,896]{1,0:T(8,128)(2,1)}, bf16[256,896]{1,0:T(8,128)(2,1)S(1)}, u32[]{:S(2)}, u32[]{:S(2)}) %collective-permute-start.183) | collective-permute-done | bytes 458784 | tf_op jit(solution)/shard_map/ppermute | solution.py:720
  (1438 shorter events, 711.3 us)
Async XLA Ops:
  7.2 370.9 %all-gather.5.cloned.1.call-start = ((), (), s32[]{:S(2)}) async-start(), calls=%async_computation.8 | async-start | bytes 5505024 | tf_op jit(solution)/shard_map/all_gather | solution.py:871
  7.2 32.2 %collective-permute-start.3 = (s32[1]{0:T(128)}, s32[1]{0:T(128)}, u32[]{:S(2)}, u32[]{:S(2)}) collective-permute-start(s32[1]{0:T(128)} %param.14), channel_id=1, source_target_pairs={{0,24},{8,0},{16,8},{24,16},{1,25},{9,1},{17,9},{25,17},{2,26},{10... | collective-permute-start | bytes 20 | tf_op jit(solution)/shard_map/ppermute | solution.py:720
  16.3 28.8 %collective-permute-start = (bf16[256,896]{1,0:T(8,128)(2,1)S(1)}, bf16[256,896]{1,0:T(8,128)(2,1)S(1)}, u32[]{:S(2)}, u32[]{:S(2)}) collective-permute-start(bf16[256,896]{1,0:T(8,128)(2,1)S(1)} %get-tuple-element.728), channel_id=1, source_target_pairs={{0,8},{8,16},{16,24},{24,0},{1,9},{9,17},{17,25},{25,1},{2,10},{10... | collective-permute-start | bytes 1376264 | tf_op jit(solution)/shard_map/ppermute | solution.py:720
  69.4 45.8 %collective-permute-start.11 = (bf16[128,2048]{1,0:T(8,128)(2,1)}, bf16[128,2048]{1,0:T(8,128)(2,1)}, u32[]{:S(2)}, u32[]{:S(2)}) collective-permute-start(bf16[128,2048]{1,0:T(8,128)(2,1)} %get-tuple-element.747.refs_0_), channel_id=1, source_target_pairs={{0,8},{8,16},{16,24},{24,0},{1,9},{9,17},{17,25},{25,1},{2,10},{10... | collective-permute-start | bytes 1572872 | tf_op jit(solution)/shard_map/ppermute | solution.py:720
  232.3 35.1 %collective-permute-start.41 = (bf16[128,2048]{1,0:T(8,128)(2,1)S(1)}, bf16[128,2048]{1,0:T(8,128)(2,1)S(1)}, u32[]{:S(2)}, u32[]{:S(2)}) collective-permute-start(bf16[128,2048]{1,0:T(8,128)(2,1)S(1)} %add_convert_fusion.26), channel_id=1, source_target_pairs={{16,8},{24,16},{17,9},{25,17},{18,10},{26,18},{19,11},{27,19},{20,... | collective-permute-start | bytes 1572872 | tf_op jit(solution)/shard_map/ppermute | solution.py:792
  233.0 34.4 %collective-permute-start.45 = (bf16[128,2048]{1,0:T(8,128)(2,1)S(1)}, bf16[128,2048]{1,0:T(8,128)(2,1)S(1)}, u32[]{:S(2)}, u32[]{:S(2)}) collective-permute-start(bf16[128,2048]{1,0:T(8,128)(2,1)S(1)} %add_convert_fusion.26), channel_id=1, source_target_pairs={{0,8},{8,16},{1,9},{9,17},{2,10},{10,18},{3,11},{11,19},{4,12},{12... | collective-permute-start | bytes 1572872 | tf_op jit(solution)/shard_map/ppermute | solution.py:791
  238.1 29.4 %collective-permute-start.42 = (bf16[128,2048]{1,0:T(8,128)(2,1)S(1)}, bf16[128,2048]{1,0:T(8,128)(2,1)S(1)}, u32[]{:S(2)}, u32[]{:S(2)}) collective-permute-start(bf16[128,2048]{1,0:T(8,128)(2,1)S(1)} %add_convert_fusion.25), channel_id=1, source_target_pairs={{0,2},{1,3},{2,0},{3,1},{4,6},{5,7},{6,4},{7,5},{8,10},{9,11},{10,... | collective-permute-start | bytes 1572872 | tf_op jit(solution)/shard_map/ppermute | solution.py:716
  249.1 32.1 %collective-permute-start.49 = (bf16[128,2048]{1,0:T(8,128)(2,1)}, bf16[128,2048]{1,0:T(8,128)(2,1)}, u32[]{:S(2)}, u32[]{:S(2)}) collective-permute-start(bf16[128,2048]{1,0:T(8,128)(2,1)} %get-tuple-element.915), channel_id=1, source_target_pairs={{0,1},{1,0},{2,3},{3,2},{4,5},{5,4},{6,7},{7,6},{8,9},{9,8},{10,11... | collective-permute-start | bytes 1572872 | tf_op jit(solution)/shard_map/ppermute | solution.py:716
  271.6 159.9 %all-gather.7.cloned.1.call-start = ((), (), s32[]{:S(2)}) async-start(), calls=%async_computation.9 | async-start | bytes 3932160 | tf_op jit(solution)/shard_map/all_gather | solution.py:871
  364.8 239.6 %reduce-scatter.7.cloned.1.call-start = ((), (), s32[]{:S(2)}) async-start(), calls=%async_computation.5 | async-start | bytes 3932160 | tf_op jit(solution)/shard_map/reduce_scatter | solution.py:880
  412.5 41.2 %collective-permute-start.74 = (bf16[128,2048]{1,0:T(8,128)(2,1)}, bf16[128,2048]{1,0:T(8,128)(2,1)}, u32[]{:S(2)}, u32[]{:S(2)}) collective-permute-start(bf16[128,2048]{1,0:T(8,128)(2,1)} %get-tuple-element.983.refs_0_), channel_id=1, source_target_pairs={{0,8},{8,16},{16,24},{24,0},{1,9},{9,17},{17,25},{25,1},{2,10},{10... | collective-permute-start | bytes 1572872 | tf_op jit(solution)/shard_map/ppermute | solution.py:720
  524.4 189.8 %reduce-scatter.5.cloned.1.call-start = ((), (), s32[]{:S(2)}) async-start(), calls=%async_computation.4 | async-start | bytes 5505024 | tf_op jit(solution)/shard_map/reduce_scatter | solution.py:880
  596.7 314.7 %reduce-scatter.9.cloned.1.call-start = ((), (), s32[]{:S(2)}) async-start(), calls=%async_computation.6 | async-start | bytes 3932160 | tf_op jit(solution)/shard_map/reduce_scatter | solution.py:880
  651.9 31.1 %collective-permute-start.118 = (bf16[128,2048]{1,0:T(8,128)(2,1)S(1)}, bf16[128,2048]{1,0:T(8,128)(2,1)S(1)}, u32[]{:S(2)}, u32[]{:S(2)}) collective-permute-start(bf16[128,2048]{1,0:T(8,128)(2,1)S(1)} %collective-permute-done.112.refs_0_.refs_4_), channel_id=1, source_target_pairs={{0,2},{1,3},{2,0},{3,1},{4,6},{5,7},{6,4},{7,5},{8,10},{9,11},{10,... | collective-permute-start | bytes 1572872 | tf_op jit(solution)/shard_map/ppermute | solution.py:716
  652.3 30.8 %collective-permute-start.119 = (bf16[128,2048]{1,0:T(8,128)(2,1)S(1)}, bf16[128,2048]{1,0:T(8,128)(2,1)S(1)}, u32[]{:S(2)}, u32[]{:S(2)}) collective-permute-start(bf16[128,2048]{1,0:T(8,128)(2,1)S(1)} %collective-permute-done.112.refs_0_.refs_4_), channel_id=1, source_target_pairs={{0,1},{1,0},{2,3},{3,2},{4,5},{5,4},{6,7},{7,6},{8,9},{9,8},{10,11... | collective-permute-start | bytes 1572872 | tf_op jit(solution)/shard_map/ppermute | solution.py:716
  652.3 30.0 %collective-permute-start.116 = (bf16[256,640]{1,0:T(8,128)(2,1)S(1)}, bf16[256,640]{1,0:T(8,128)(2,1)S(1)}, u32[]{:S(2)}, u32[]{:S(2)}) collective-permute-start(bf16[256,640]{1,0:T(8,128)(2,1)S(1)} %get-tuple-element.1173), channel_id=1, source_target_pairs={{0,16},{8,24},{16,0},{24,8},{1,17},{9,25},{17,1},{25,9},{2,18},{10... | collective-permute-start | bytes 983048 | tf_op jit(solution)/shard_map/ppermute | solution.py:720
  731.0 31.7 %collective-permute-start.134 = (bf16[128,2048]{1,0:T(8,128)(2,1)S(1)}, bf16[128,2048]{1,0:T(8,128)(2,1)S(1)}, u32[]{:S(2)}, u32[]{:S(2)}) collective-permute-start(bf16[128,2048]{1,0:T(8,128)(2,1)S(1)} %copy-done.197), channel_id=1, source_target_pairs={{0,1},{1,0},{2,3},{3,2},{4,5},{5,4},{6,7},{7,6},{8,9},{9,8},{10,11... | collective-permute-start | bytes 1572872 | tf_op jit(solution)/shard_map/ppermute | solution.py:716
  766.4 31.1 %collective-permute-start.139 = (bf16[128,2048]{1,0:T(8,128)(2,1)S(1)}, bf16[128,2048]{1,0:T(8,128)(2,1)S(1)}, u32[]{:S(2)}, u32[]{:S(2)}) collective-permute-start(bf16[128,2048]{1,0:T(8,128)(2,1)S(1)} %add_convert_fusion.12), channel_id=1, source_target_pairs={{16,8},{24,16},{17,9},{25,17},{18,10},{26,18},{19,11},{27,19},{20,... | collective-permute-start | bytes 1572872 | tf_op jit(solution)/shard_map/ppermute | solution.py:792
  808.1 170.3 %reduce-scatter.11.cloned.1.call-start = ((), (), s32[]{:S(2)}) async-start(), calls=%async_computation.7 | async-start | bytes 5505024 | tf_op jit(solution)/shard_map/reduce_scatter | solution.py:880
  852.8 38.1 %collective-permute-start.164 = (bf16[128,2048]{1,0:T(8,128)(2,1)}, bf16[128,2048]{1,0:T(8,128)(2,1)}, u32[]{:S(2)}, u32[]{:S(2)}) collective-permute-start(bf16[128,2048]{1,0:T(8,128)(2,1)} %get-tuple-element.1337), channel_id=1, source_target_pairs={{0,1},{1,0},{2,3},{3,2},{4,5},{5,4},{6,7},{7,6},{8,9},{9,8},{10,11... | collective-permute-start | bytes 1572872 | tf_op jit(solution)/shard_map/ppermute | solution.py:716
  862.2 30.3 %collective-permute-start.165 = (bf16[128,2048]{1,0:T(8,128)(2,1)}, bf16[128,2048]{1,0:T(8,128)(2,1)S(1)}, u32[]{:S(2)}, u32[]{:S(2)}) collective-permute-start(bf16[128,2048]{1,0:T(8,128)(2,1)} %reshape.334), channel_id=1, source_target_pairs={{0,2},{1,3},{2,0},{3,1},{4,6},{5,7},{6,4},{7,5},{8,10},{9,11},{10,... | collective-permute-start | bytes 1572872 | tf_op jit(solution)/shard_map/ppermute | solution.py:716
  862.9 30.4 %collective-permute-start.166 = (bf16[128,2048]{1,0:T(8,128)(2,1)}, bf16[128,2048]{1,0:T(8,128)(2,1)S(1)}, u32[]{:S(2)}, u32[]{:S(2)}) collective-permute-start(bf16[128,2048]{1,0:T(8,128)(2,1)} %reshape.334), channel_id=1, source_target_pairs={{0,1},{1,0},{2,3},{3,2},{4,5},{5,4},{6,7},{7,6},{8,9},{9,8},{10,11... | collective-permute-start | bytes 1572872 | tf_op jit(solution)/shard_map/ppermute | solution.py:716
  903.0 51.4 %collective-permute-start.167 = (bf16[128,2048]{1,0:T(8,128)(2,1)}, bf16[128,2048]{1,0:T(8,128)(2,1)}, u32[]{:S(2)}, u32[]{:S(2)}) collective-permute-start(bf16[128,2048]{1,0:T(8,128)(2,1)} %copy-done.404), channel_id=1, source_target_pairs={{0,1},{1,0},{2,3},{3,2},{4,5},{5,4},{6,7},{7,6},{8,9},{9,8},{10,11... | collective-permute-start | bytes 1572872 | tf_op jit(solution)/shard_map/ppermute | solution.py:716
  956.2 49.0 %collective-permute-start.175 = (bf16[128,2048]{1,0:T(8,128)(2,1)}, bf16[128,2048]{1,0:T(8,128)(2,1)}, u32[]{:S(2)}, u32[]{:S(2)}) collective-permute-start(bf16[128,2048]{1,0:T(8,128)(2,1)} %collective-permute-done.172), channel_id=1, source_target_pairs={{0,1},{1,0},{2,3},{3,2},{4,5},{5,4},{6,7},{7,6},{8,9},{9,8},{10,11... | collective-permute-start | bytes 1572872 | tf_op jit(solution)/shard_map/ppermute | solution.py:716
  (592 other events, 5909.1 us)
Sparse Core Ops, SparseCore 0:
  271.7 55.4 all-gather.4
  365.0 45.8 all-gather.6
  524.6 49.6 reduce-scatter.6
  596.9 54.4 reduce-scatter.4
  808.2 38.5 reduce-scatter.8
  894.3 49.2 reduce-scatter.10

commit v2 on v1

--- a/solution.py
+++ b/solution.py
@@ -424,10 +424,9 @@
         for j in range(got_ref.shape[0]):
             gkv = gkv + got_ref[j, at, :].astype(F32)
         gkey = turn(gkv[:, :n], table_ref[:, at], back=True).astype(BF16)
-        gin = jnp.concatenate(
-            [gq_ref[at, :], gkey, gkv[:, n:].astype(BF16), gup_ref[at, :]], axis=1
-        )
+        gin = jnp.concatenate([gq_ref[at, :], gkey, gkv[:, n:].astype(BF16)], axis=1)
         gin_ref[at, :] = gin
+        gin = jnp.concatenate([gin, gup_ref[at, :]], axis=1)
         out = dot(gin, w_ref[...], NT).astype(BF16)
         for j in range(half):
             y_refs[part * half + j][...] = out[j * rows : (j + 1) * rows]
@@ -437,12 +436,12 @@
 
 
 def in_back(gq, gkv, got, gup, win, tables, rows):
-    run = gq.shape[0]
+    run, n = gq.shape
     width, wide = win.shape
     shape = jax.ShapeDtypeStruct
     return pl.pallas_call(
         in_back_kernel,
-        out_shape=[shape((run, wide), BF16), shape((1, wide), F32)]
+        out_shape=[shape((run, 3 * n), BF16), shape((1, wide), F32)]
         + [shape((rows, width), BF16)] * (run // rows),
         compiler_params=plain(),
         cost_estimate=cost(2 * run * width * wide, 2 * win.size),
@@ -450,41 +449,55 @@
     )(gq, gkv, got, gup, win, tables)
 
 
-def weight_grad_kernel(count, slots, *refs):
-    xs, ys, out_ref, hold_ref = refs[:count], refs[count:-2], refs[-2], refs[-1]
-
-    @pl.when(pl.program_id(0) == 0)
+def weight_grad_kernel(counts, *refs):
+    out_ref, hold_ref = refs[-2:]
+    first = pl.program_id(0) == 0
+    groups = []
+    col = at = 0
+    for xs, slots, parts in counts:
+        groups.append((refs[at : at + xs], refs[at + xs : at + xs + slots * parts], slots, col))
+        for j in range(parts):
+            col += refs[at + xs + j * slots].shape[1]
+        at += xs + slots * parts
+
+    @pl.when(first)
     def _():
-        col = 0
-        for j in range(len(ys) // slots):
-            for m in range(slots):
-                y_ref = ys[j * slots + m]
-                run, wide = y_ref.shape
-                hold_ref[m * run : (m + 1) * run, col : col + wide] = y_ref[...]
-            col += wide
-
-    left = jnp.concatenate([ref[...] for ref in xs], axis=0)
-    out_ref[...] = dot(left, hold_ref[...], TN).astype(BF16)
-
-
-def weight_grad(xs, ys, block):
-    rows, width = xs[0].shape
-    tokens = rows * len(xs)
-    slots = len(ys[0])
-    wide = sum(part[0].shape[1] for part in ys)
-    flat = [array for part in ys for array in part]
+        for _, ys, slots, col in groups:
+            for j in range(len(ys) // slots):
+                for m in range(slots):
+                    y_ref = ys[j * slots + m]
+                    run, wide = y_ref.shape
+                    hold_ref[m * run : (m + 1) * run, col : col + wide] = y_ref[...]
+                col += ys[j * slots].shape[1]
+
+    for k, (xs, _, _, col) in enumerate(groups):
+        end = groups[k + 1][3] if k + 1 < len(groups) else out_ref.shape[1]
+        left = jnp.concatenate([ref[...] for ref in xs], axis=0)
+        out_ref[:, col:end] = dot(left, hold_ref[:, col:end], TN).astype(BF16)
+
+
+def weight_grad(groups, block):
+    rows, width = groups[0][0][0].shape
+    tokens = rows * len(groups[0][0])
+    counts, specs, flat = [], [], []
+    for xs, ys in groups:
+        counts.append((len(xs), len(ys[0]), len(ys)))
+        arrays = [array for part in ys for array in part]
+        specs += [pl.BlockSpec((rows, block), lambda i: (0, i)) for _ in xs]
+        specs += [whole(*array.shape) for array in arrays]
+        flat += [*xs, *arrays]
+    wide = sum(part[0].shape[1] for _, ys in groups for part in ys)
     return pl.pallas_call(
-        functools.partial(weight_grad_kernel, len(xs), slots),
+        functools.partial(weight_grad_kernel, tuple(counts)),
         grid=(width // block,),
-        in_specs=[pl.BlockSpec((rows, block), lambda i: (0, i)) for _ in xs]
-        + [whole(*array.shape) for array in flat],
+        in_specs=specs,
         out_specs=rows_of(block, wide),
         out_shape=jax.ShapeDtypeStruct((width, wide), BF16),
         scratch_shapes=[pltpu.VMEM((tokens, wide), BF16)],
         compiler_params=params(),
         cost_estimate=cost(2 * tokens * width * wide, 2 * tokens * (width + wide)),
         name="weight_grad",
-    )(*xs, *flat)
+    )(*flat)
 
 
 def at_part(index, size):
@@ -529,51 +542,53 @@
 
 def place_kernel(count, at_ref, *refs):
     blocks, out_ref, sems = refs[:count], refs[count], refs[count + 1]
-    copies = [
-        pltpu.make_async_copy(blocks[k], out_ref.at[at_ref[k]], sems.at[k]) for k in range(count)
-    ]
+    copies = []
+    for k, block_ref in enumerate(blocks):
+        rows = pl.ds(pl.multiple_of(at_ref[k], 16), block_ref.shape[0])
+        copies.append(pltpu.make_async_copy(block_ref, out_ref.at[rows], sems.at[k]))
     for copy in copies:
         copy.start()
     for copy in copies:
         copy.wait()
 
 
-def place(places, blocks):
+def place(rows, blocks):
     count = len(blocks)
+    total = sum(block.shape[0] for block in blocks)
     return pl.pallas_call(
         functools.partial(place_kernel, count),
         in_specs=[pl.BlockSpec(memory_space=pltpu.SMEM)]
         + [pl.BlockSpec(memory_space=pltpu.VMEM)] * count,
         out_specs=pl.BlockSpec(memory_space=pl.ANY),
-        out_shape=jax.ShapeDtypeStruct((count, *blocks[0].shape), BF16),
+        out_shape=jax.ShapeDtypeStruct((total, blocks[0].shape[1]), BF16),
         scratch_shapes=[pltpu.SemaphoreType.DMA((count,))],
         compiler_params=plain(),
         cost_estimate=COST,
         name="place",
-    )(jnp.stack(places), *blocks)
-
-
-def unpack_in_kernel(held, at_ref, *refs):
-    blocks, (qkv_ref, up_ref) = refs[: -2 - held], refs[-2:]
+    )(rows, *blocks)
+
+
+def unpack_qkv_kernel(held, at_ref, *refs):
+    blocks, qkv_ref = refs[: -1 - held], refs[-1]
     count = len(blocks)
-    n, f = qkv_ref.shape[3] // count, up_ref.shape[2] // count
+    n = qkv_ref.shape[3] // count
     for k, block_ref in enumerate(blocks):
         source = (at_ref[0] + count - k) % count
         value = block_ref[...].astype(F32)
         for j in range(3):
             qkv_ref[0, j, :, at_part(source, n)] = value[:, j * n : (j + 1) * n]
-        up_ref[0, :, at_part(source, f)] = value[:, 3 * n :]
-
-
-def unpack_out_kernel(held, at_ref, *refs):
-    blocks, (out_ref, down_ref) = refs[: -2 - held], refs[-2:]
+
+
+def unpack_rest_kernel(held, at_ref, *refs):
+    blocks, (out_ref, down_ref, up_ref) = refs[: -3 - held], refs[-3:]
     count = len(blocks)
     n, f = out_ref.shape[1] // count, down_ref.shape[1] // count
     for k, block_ref in enumerate(blocks):
         source = (at_ref[0] + count - k) % count
         value = block_ref[...].astype(F32)
         out_ref[0, at_part(source, n), :] = value[:, :n].T
-        down_ref[0, at_part(source, f), :] = value[:, n:].T
+        down_ref[0, at_part(source, f), :] = value[:, n : n + f].T
+        up_ref[0, :, at_part(source, f)] = value[:, n + f :]
 
 
 def unpack(kernel, at, blocks, layer, shapes, held):
@@ -597,30 +612,106 @@
     )(at, *blocks, *held)
 
 
-def norm_kernel(count, *refs):
+def blocks_in_order(array, outer, inner):
+    d = array.shape[-1] // (outer * inner)
+    places = [(i * inner + j) * d for j in range(inner) for i in range(outer)]
+    return jnp.concatenate([array[..., p : p + d] for p in places], axis=-1)
+
+
+def first_kernel(S, C, at_ref, x_ref, gain_ref, shift_ref, hidden_ref, *out_refs):
+    rows = hidden_ref.shape[0]
+    gain, shift = (blocks_in_order(ref[...], S, C) for ref in (gain_ref, shift_ref))
+    for b, out_ref in enumerate(out_refs):
+        x = x_ref[0, at_part(at_ref[1] ^ b, rows), :].astype(F32)
+        x = blocks_in_order(x, S, C)
+        if b == 0:
+            hidden_ref[...] = x
+        out_ref[...] = layer_norm(x, gain, shift).astype(BF16)
+
+
+def first_norm(at, x, gain, shift, S, C, count):
+    rows, width = x.shape[1] // count, x.shape[2]
+    shape = jax.ShapeDtypeStruct
+    vmem = pl.BlockSpec(memory_space=pltpu.VMEM)
+    return pl.pallas_call(
+        functools.partial(first_kernel, S, C),
+        in_specs=[pl.BlockSpec(memory_space=pltpu.SMEM), vmem, vmem, vmem],
+        out_shape=[shape((rows, width), F32)] + [shape((rows, width), BF16)] * count,
+        compiler_params=plain(),
+        cost_estimate=COST,
+        name="first_norm",
+    )(at, x, gain[None], shift[None])
+
+
+def last_kernel(S, C, at_ref, x_ref, grad_ref, *out_refs):
+    rows = grad_ref.shape[0]
+    for b, out_ref in enumerate(out_refs):
+        part = at_ref[1] ^ b
+        x = blocks_in_order(x_ref[0, at_part(part, rows), :].astype(F32), S, C)
+        at = at_ref[0] * len(out_refs) * rows + part * rows
+        at = at + lax.broadcasted_iota(jnp.int32, (rows, 1), 0)
+        x = jnp.where(at < at_ref[2], x, 0.0)
+        if b == 0:
+            grad_ref[...] = x
+        out_ref[...] = x.astype(BF16)
+
+
+def last_grad(at, x, S, C, count):
+    rows, width = x.shape[1] // count, x.shape[2]
+    shape = jax.ShapeDtypeStruct
+    return pl.pallas_call(
+        functools.partial(last_kernel, S, C),
+        in_specs=[pl.BlockSpec(memory_space=pltpu.SMEM), pl.BlockSpec(memory_space=pltpu.VMEM)],
+        out_shape=[shape((rows, width), F32)] + [shape((rows, width), BF16)] * count,
+        compiler_params=plain(),
+        cost_estimate=COST,
+        name="last_grad",
+    )(at, x)
+
+
+def rows_kernel(S, C, at_ref, x_ref, out_ref):
+    rows = x_ref.shape[0]
+    at = at_ref[0] + lax.broadcasted_iota(jnp.int32, (rows, 1), 0)
+    x = jnp.where(at < at_ref[1], x_ref[...].astype(F32), 0.0)
+    out_ref[...] = blocks_in_order(x, C, S).astype(BF16)
+
+
+def rows_out(at, x, S, C):
+    return pl.pallas_call(
+        functools.partial(rows_kernel, S, C),
+        in_specs=[pl.BlockSpec(memory_space=pltpu.SMEM), pl.BlockSpec(memory_space=pltpu.VMEM)],
+        out_shape=jax.ShapeDtypeStruct(x.shape, BF16),
+        compiler_params=plain(),
+        cost_estimate=COST,
+        name="rows_out",
+    )(at, x)
+
+
+def norm_kernel(count, S, C, *refs):
     parts = refs[:count]
-    hidden_ref, bias_ref, gain_ref, shift_ref, next_ref, normed_ref = refs[count:]
-    hidden = hidden_ref[...] + bias_ref[...]
+    hidden_ref, out_ref, down_ref, gain_ref, shift_ref, next_ref, normed_ref = refs[count:]
+    hidden = hidden_ref[...] + blocks_in_order(out_ref[...] + down_ref[...], S, C)
     for ref in parts:
         hidden = hidden + ref[...].astype(F32)
     next_ref[...] = hidden
-    normed_ref[...] = layer_norm(hidden, gain_ref[...], shift_ref[...]).astype(BF16)
-
-
-def sum_norm(parts, hidden, bias, gain, shift):
+    gain, shift = (blocks_in_order(ref[...], S, C) for ref in (gain_ref, shift_ref))
+    normed_ref[...] = layer_norm(hidden, gain, shift).astype(BF16)
+
+
+def sum_norm(parts, hidden, rows, S, C):
     shape = jax.ShapeDtypeStruct
     return pl.pallas_call(
-        functools.partial(norm_kernel, len(parts)),
+        functools.partial(norm_kernel, len(parts), S, C),
         out_shape=[shape(hidden.shape, F32), shape(hidden.shape, BF16)],
         compiler_params=plain(),
         cost_estimate=COST,
         name="sum_norm",
-    )(*parts, hidden, bias[None], gain[None], shift[None])
-
-
-def norm_back_kernel(count, *refs):
+    )(*parts, hidden, *[row[None] for row in rows])
+
+
+def norm_back_kernel(count, S, C, *refs):
     parts = refs[:count]
-    hidden_ref, grad_ref, gain_ref, next_ref, low_ref, ggain_ref, gshift_ref = refs[count:]
+    hidden_ref, grad_ref, gain_ref, next_ref, low_ref, sums_ref = refs[count:]
     total = parts[0][...].astype(F32)
     for ref in parts[1:]:
         total = total + ref[...].astype(F32)
@@ -628,22 +719,26 @@
     centred = hidden - jnp.mean(hidden, -1, keepdims=True)
     factor = lax.rsqrt(jnp.mean(centred * centred, -1, keepdims=True) + 1e-05)
     xhat = centred * factor
-    ggain_ref[...] = jnp.sum(total * xhat, 0, keepdims=True)
-    gshift_ref[...] = jnp.sum(total, 0, keepdims=True)
-    inner = total * gain_ref[...]
+    grad = grad_ref[...]
+    for j, value in enumerate((total * xhat, total, grad)):
+        sums_ref[j : j + 1, :] = blocks_in_order(jnp.sum(value, 0, keepdims=True), C, S)
+    inner = total * blocks_in_order(gain_ref[...], S, C)
     first = jnp.mean(inner, -1, keepdims=True)
     second = jnp.mean(inner * xhat, -1, keepdims=True)
-    grad = grad_ref[...] + factor * (inner - first - xhat * second)
+    grad = grad + factor * (inner - first - xhat * second)
     next_ref[...] = grad
     low_ref[...] = grad.astype(BF16)
 
 
-def sum_norm_back(parts, hidden, grad, gain):
+def sum_norm_back(parts, hidden, grad, gain, S, C):
     shape = jax.ShapeDtypeStruct
-    row = shape((1, hidden.shape[1]), F32)
     return pl.pallas_call(
-        functools.partial(norm_back_kernel, len(parts)),
-        out_shape=[shape(hidden.shape, F32), shape(hidden.shape, BF16), row, row],
+        functools.partial(norm_back_kernel, len(parts), S, C),
+        out_shape=[
+            shape(hidden.shape, F32),
+            shape(hidden.shape, BF16),
+            shape((3, hidden.shape[1]), F32),
+        ],
         compiler_params=plain(),
         cost_estimate=COST,
         name="sum_norm_back",
@@ -697,6 +792,10 @@
 def until(ready):
     while not ready():
         yield WAIT
+
+
+FAST = [[(1, None), (3, None)], [(2, None)]]
+SLOW = [[(1, None)], [(3, None)], [(2, 0)], [(2, 1)]]
 
 
 class Group:
@@ -833,45 +932,51 @@
             lax.ppermute(block, "ctx", [(i, (i + j) % C) for i in range(C)]) for j in range(1, C)
         ]
 
-    def gather_weights(self, pieces, done, sent):
+    def gather_weights(self, pieces, done, sent, rounds):
         S, C = self.S, self.C
         d, wide = pieces[0].shape
-        blocks, places = [pieces[0]], [0]
-        others = []
-        for shifts, back in (([1, 3], [0]), ([2], [1, 3]), ([], [2])):
-            ready = dict(zip(places, blocks))
-            got = [self.shift(pieces[k], k) for k in shifts]
-            new = [self.ctx_others(ready[k]) for k in back]
-            got, new, blocks, others, pieces = yield got, new, blocks, others, pieces
-            blocks, places = blocks + got, places + shifts
-            others = others + list(zip(back, new))
-            if shifts == [2]:
+        back = [(pieces[0], 0, 0)]
+        blocks, starts = [], []
+        rounds = list(rounds)
+        while back or rounds:
+            shifts = rounds.pop(0) if rounds else []
+            parts = []
+            for k, part in shifts:
+                piece = pieces[k]
+                if part is not None:
+                    piece = piece[part * d // 2 : (part + 1) * d // 2]
+                parts.append((piece, k, 0 if part is None else part * d // 2))
+            got = [self.shift(piece, k) for piece, k, _ in parts]
+            others = [self.ctx_others(block) for block, _, _ in back]
+            got, others, blocks, pieces = yield got, others, blocks, pieces
+            blocks = list(blocks)
+            for (block, k, row), found in zip(back, others):
+                for j, part in enumerate([block] + list(found)):
+                    blocks.append(part)
+                    starts.append((j, k, row))
+            back = [(block, k, row) for block, (_, k, row) in zip(got, parts)]
+            if not rounds:
                 sent()
-        flat, at = [], []
-        for k, block in zip(places, blocks):
-            flat.append(block)
-            at.append(self.c * S + (self.s - k) % S)
-        for k, found in others:
-            for j, block in enumerate(found):
-                flat.append(block)
-                at.append((self.c - j - 1) % C * S + (self.s - k) % S)
-        done(place(at, flat).reshape(C * S * d, wide))
+        j, k, row = jnp.asarray(starts, jnp.int32).T
+        done(place(((self.c - j) % C * S + (self.s - k) % S) * d + row, blocks))
 
     def gather_weights_later(self, pieces, done, sent, steps):
         S, C = self.S, self.C
         d, wide = pieces[0].shape
-        first, pieces = yield [self.shift(pieces[1], 1)], pieces
-        more, first, pieces = yield [self.shift(pieces[3], 3)], first, pieces
-        first = first + more
-        second, first, pieces = yield [self.shift(pieces[2], 2)], first, pieces
+        got = []
+        for k, piece in ((1, pieces[1]), (3, pieces[3])) + self.halves(pieces[2]):
+            got, pieces = yield got + [self.shift(piece, k)], pieces
         sent()
-        flat = place(
-            [(self.s - k) % S for k in (0, 1, 3, 2)], [pieces[0], first[0], first[1], second[0]]
-        )
+        k, row = jnp.asarray([(0, 0), (1, 0), (3, 0), (2, 0), (2, d // 2)], jnp.int32).T
+        flat = place((self.s - k) % S * d + row, [pieces[0], *got])
         array = lax.all_gather(flat, "ctx")
         for _ in range(steps):
             yield ()
         done(array.reshape(C * S * d, wide))
+
+    def halves(self, block):
+        half = block.shape[0] // 2
+        return ((2, block[:half]), (2, block[half:]))
 
     def scatter_weights(self, grad, done, steps):
         S, C = self.S, self.C
@@ -883,28 +988,61 @@
         pieces = [
             lax.dynamic_index_in_dim(own, (self.s + k) % S, 0, keepdims=False) for k in range(S)
         ]
-        first, pieces = yield [self.shift(pieces[1], 1)], pieces
-        more, first, pieces = yield [self.shift(pieces[3], 3)], first, pieces
-        first = first + more
-        second, first, pieces = yield [self.shift(pieces[2], 2)], first, pieces
-        done([pieces[0], first[0], second[0], first[1]])
+        got = []
+        for k, piece in ((1, pieces[1]), (3, pieces[3])) + self.halves(pieces[2]):
+            got, pieces = yield got + [self.shift(piece, k)], pieces
+        done([pieces[0], got[0], jnp.concatenate(got[2:]), got[1]])
+
+    def scatter_weights_now(self, grad, done, slow=False):
+        S, C = self.S, self.C
+        wide = grad.shape[1]
+        d = grad.shape[0] // (S * C)
+        grad = grad.reshape(C, S, d, wide)
+
+        def piece(k, j):
+            at = ((self.c + j) % C, (self.s + k) % S, 0, 0)
+            return lax.dynamic_slice(grad, at, (1, 1, d, wide)).reshape(d, wide)
+
+        def add(k):
+            other = [
+                lax.ppermute(piece(k, j), "ctx", [(i, (i + j) % C) for i in range(C)])
+                for j in range(1, C)
+            ]
+            return [piece(k, 0)] + other
+
+        def total(parts):
+            value = sum((part.astype(F32) for part in parts[1:]), parts[0].astype(F32))
+            return lax.optimization_barrier(value.astype(BF16))
+
+        if slow:
+            two, one = yield add(2), add(1)
+            low, high = self.halves(total(two))
+            low, high, one, three = yield self.shift(low[1], 2), high[1], one, add(3)
+            low, high, one, three, own = yield low, self.shift(high, 2), one, three, add(0)
+            low, high, one, three, own = yield low, high, self.shift(total(one), 1), three, own
+            low, high, one, three, own = yield (
+                low, high, one, self.shift(total(three), 3), total(own),
+            )
+            done([own, one, jnp.concatenate([low, high]), three])
+            return
+        two, one = yield add(2), add(1)
+        two, one, three, own = yield self.shift(total(two), 2), self.shift(total(one), 1), add(3), add(0)
+        two, one, three, own = yield two, one, self.shift(total(three), 3), total(own)
+        done([own, one, two, three])
 
     def add_up(self, small, part, finish):
         cut = small.shape[0]
         both = jnp.concatenate([small, part])
-        for axis, size in (("slot", self.S), ("ctx", self.C)):
-            bit = 1
-            while bit < size:
-                got = lax.ppermute(both, axis, [(i, i ^ bit) for i in range(size)])
-                got, both = yield got, both
-                both = both + got
-                bit *= 2
+        got = [self.shift(both, k) for k in range(1, self.S)]
+        got, both = yield got, both
+        both = sum(got, both)
+        got = self.ctx_others(both)
+        got, both = yield got, both
+        both = sum(got, both)
         small, part = both[:cut], both[cut:]
-        for bit in (self.far, self.near):
-            got = self.swap(small, bit)
-            got, small, part = yield got, small, part
-            small = small + got
-        finish(small, part)
+        got = [self.swap(small, bit) for bit in range(1, self.T)]
+        got, small, part = yield got, small, part
+        finish(sum(got, small), part)
 
 
 def on_device(
@@ -932,22 +1070,11 @@
     block = run // 2
     stages = Stages(lengths)
 
-    def to_held(array):
-        lead = array.shape[:-1]
-        return array.reshape(*lead, S, C, d).swapaxes(-3, -2).reshape(*lead, width)
-
-    def from_held(array):
-        lead = array.shape[:-1]
-        return array.reshape(*lead, C, S, d).swapaxes(-3, -2).reshape(*lead, width)
-
-    inputs, cotangent = to_held(inputs), to_held(cotangent)
-    ln_gain, ln_shift = to_held(ln_gain), to_held(ln_shift)
-    b_out, b_down = to_held(b_out), to_held(b_down)
+    here = jnp.concatenate([grp.c[None], grp.corner[None], lengths]).astype(jnp.int32)
+    own_at = jnp.concatenate([(grp.c * run + grp.corner * rows)[None], lengths]).astype(jnp.int32)
     local = jnp.arange(run, dtype=jnp.int32)
     positions = grp.c * run + (local // rows ^ grp.corner) * rows + local % rows
     tables = rotary_tables(positions, n // HD)
-    valid = (positions < lengths[0]).astype(F32)[:, None]
-    own_valid = valid[:rows]
     box = {}
     kept = [[None] * S for _ in range(LAYERS)]
     normed = [[None] * S for _ in range(LAYERS)]
@@ -982,7 +1109,9 @@
         )
         pieces = list(stages.hold(*pieces))
         if later is None:
-            yield from grp.gather_weights(pieces, mark("win", layer), mark("win sent", layer))
+            yield from grp.gather_weights(
+                pieces, mark("win", layer), mark("win sent", layer), FAST if layer == 0 else SLOW
+            )
         else:
             yield from grp.gather_weights_later(
                 pieces, mark("win", layer), mark("win sent", layer), later
@@ -993,7 +1122,9 @@
         pieces = pack(pack_out_kernel, grp.slot_at, w_out, w_down, layer, (d, n + f), S)
         pieces = list(stages.hold(*pieces))
         if later is None:
-            yield from grp.gather_weights(pieces, mark("wout", layer), mark("wout sent", layer))
+            yield from grp.gather_weights(
+                pieces, mark("wout", layer), mark("wout sent", layer), FAST if layer == 0 else SLOW
+            )
         else:
             yield from grp.gather_weights_later(
                 pieces, mark("wout", layer), mark("wout sent", layer), later
@@ -1003,12 +1134,13 @@
         yield from after(("win", layer), ("at", k))
         normed[layer][k] = parts
         q, kv, up, act = in_project(parts, box["win", layer], biases[layer], tables, n)
-        if k == 2:
-            prev = grp.ctx_before(kv)
+        prev = grp.ctx_before(kv)
+        if k != 2:
             q, kv, up, act = yield q, kv, up, act
         else:
-            q, kv, up, act = yield q, kv, up, act
-            q, kv, up, act, prev = yield q, kv, up, act, grp.ctx_before(kv)
+            yield ()
+        if k != 2:
+            yield ()
         res, att, lse = attend(box["at", k], q, kv, prev, block, rows)
         box["attended", layer, k] = True
         kept[layer][k] = (q, kv, prev, up, act, res, att, lse)
@@ -1058,31 +1190,41 @@
     def slot_ready(kind, layer):
         return lambda m, parts: stages.spawn(kind(layer, m, parts))
 
-    def out_grads(layer, *keys, steps=4):
+    def rest_grads(layer, *keys, steps=4):
         yield from after(*keys)
         grad = weight_grad(
-            [part for parts in grad_branch[layer] for part in parts],
-            [[kept[layer][k][6] for k in range(S)], [kept[layer][k][4] for k in range(S)]],
+            [
+                (
+                    [part for parts in grad_branch[layer] for part in parts],
+                    [[kept[layer][k][6] for k in range(S)], [kept[layer][k][4] for k in range(S)]],
+                ),
+                (
+                    [part for parts in normed[layer] for part in parts],
+                    [[middle[layer][k][3] for k in range(S)]],
+                ),
+            ],
             block,
         )
-        (grad,) = yield (grad,)
-        yield from grp.scatter_weights(grad, mark("grad out", layer), steps)
-
-    def in_grads(layer, *keys, steps=4):
-        yield from after(*keys, *[("gin", layer, k) for k in range(S)])
+        yield ()
+        if layer == 0:
+            yield from grp.scatter_weights_now(grad, mark("grad rest", layer), slow=True)
+        else:
+            yield from grp.scatter_weights(grad, mark("grad rest", layer), steps)
+
+    def qkv_grads(layer, steps=4):
+        yield from after(*[("gin", layer, k) for k in range(S)])
         grad = weight_grad(
-            [part for parts in normed[layer] for part in parts], [gins[layer]], block
+            [([part for parts in normed[layer] for part in parts], [gins[layer]])], block
         )
         (grad,) = yield (grad,)
-        yield from grp.scatter_weights(grad, mark("grad in", layer), steps)
+        if layer == 0:
+            yield from grp.scatter_weights_now(grad, mark("grad qkv", layer))
+        else:
+            yield from grp.scatter_weights(grad, mark("grad qkv", layer), steps)
 
     def first_gather(*keys):
         yield from after(*keys)
-        own_rows = grp.parts_of(inputs[0], rows)
-        parts = [
-            layer_norm(part.astype(F32), ln_gain[0], ln_shift[0]).astype(BF16) for part in own_rows
-        ]
-        box["hidden", 0] = own_rows[0].astype(F32)
+        box["hidden", 0], *parts = first_norm(here, inputs, ln_gain[0], ln_shift[0], S, C, T)
         parts = list(stages.hold(*parts))
         yield from grp.gather(
             parts[0], parts, slot_ready(forward_slot, 0), mark("normed sent", 0)
@@ -1102,21 +1244,17 @@
             box["hidden", layer + 1], box["normed", layer + 1] = sum_norm(
                 parts,
                 box["hidden", layer],
-                b_out[layer] + b_down[layer],
-                ln_gain[later],
-                ln_shift[later],
+                (b_out[layer], b_down[layer], ln_gain[later], ln_shift[later]),
+                S,
+                C,
             )
 
         yield from grp.scatter(make_forward(layer), there_forward(layer), finish)
 
     def last_gradient(*keys):
         yield from after(*keys)
-        parts = [
-            part.astype(F32) * valid[b * rows : (b + 1) * rows]
-            for b, part in enumerate(grp.parts_of(cotangent[0], rows))
-        ]
-        box["grad", LAYERS] = parts[0]
-        parts = list(stages.hold(*[part.astype(BF16) for part in parts]))
+        box["grad", LAYERS], *parts = last_grad(here, cotangent, S, C, T)
+        parts = list(stages.hold(*parts))
         yield from grp.gather(
             parts[0], parts, slot_ready(backward_slot, LAYERS - 1), mark("grad sent", LAYERS)
         )
@@ -1132,11 +1270,9 @@
 
     def backward_sum(layer):
         def finish(parts):
-            grad_bias_out = jnp.sum(box["grad", layer + 1], 0)
-            box["grad", layer], box["grad low", layer], grad_gain, grad_shift = sum_norm_back(
-                parts, box["hidden", layer], box["grad", layer + 1], ln_gain[layer]
+            box["grad", layer], box["grad low", layer], small_sums[layer] = sum_norm_back(
+                parts, box["hidden", layer], box["grad", layer + 1], ln_gain[layer], S, C
             )
-            small_sums[layer] = (grad_gain[0], grad_shift[0], grad_bias_out)
 
         yield from grp.scatter(make_backward(layer), there_backward(layer), finish)
 
@@ -1154,35 +1290,40 @@
                 lax.dynamic_update_slice_in_dim(pieces, total[3 * n :], 3 * nt + grp.s * f, 0)
             )
         yield from grp.add_up(
-            jnp.concatenate([piece for entry in small_sums for piece in entry]),
+            jnp.concatenate(small_sums).reshape(-1),
             jnp.concatenate(spread),
             lambda small, part: box.__setitem__("sums", (small, part)),
         )
 
     def all_rows(key, value, name):
         yield from after(key)
-        block = from_held(value())
+        block = value()
         parts = [block, grp.swap(block, grp.far), grp.swap(block, grp.near)]
         parts = yield parts
-        box[name] = grp.in_order(list(parts) + [grp.swap(parts[1], grp.near)])[None]
-
-    def all_grads(layer, *keys):
-        yield from after(("grad in", layer), ("grad out", layer), *keys)
-        box["final in", layer] = unpack(
-            unpack_in_kernel,
+        parts = list(parts) + [grp.swap(parts[1], grp.near)]
+        starts = (grp.corner ^ jnp.arange(T, dtype=jnp.int32)) * rows
+        box[name] = place(starts, parts)[None]
+
+    def final_qkv(layer, *keys):
+        yield from after(("grad qkv", layer), *keys)
+        box["final qkv", layer] = unpack(
+            unpack_qkv_kernel,
             grp.slot_at,
-            box["grad in", layer],
+            box["grad qkv", layer],
             layer,
-            ((LAYERS, 3, d, nt), (LAYERS, d, ft)),
-            box.get(("final in", layer + 1)),
+            ((LAYERS, 3, d, nt),),
+            box.get(("final qkv", layer + 1)),
         )
-        box["final out", layer] = unpack(
-            unpack_out_kernel,
+
+    def final_rest(layer, *keys):
+        yield from after(("grad rest", layer), *keys)
+        box["final rest", layer] = unpack(
+            unpack_rest_kernel,
             grp.slot_at,
-            box["grad out", layer],
+            box["grad rest", layer],
             layer,
-            ((LAYERS, nt, d), (LAYERS, ft, d)),
-            box.get(("final out", layer + 1)),
+            ((LAYERS, nt, d), (LAYERS, ft, d), (LAYERS, d, ft)),
+            box.get(("final rest", layer + 1)),
         )
 
     last = LAYERS - 1
@@ -1192,35 +1333,36 @@
     stages.spawn(forward_sum(0))
     stages.spawn(out_weights(0, ("normed sent", 0)))
     for layer in range(1, LAYERS):
-        stages.spawn(in_weights(layer, ("wout", layer - 1), later=3))
+        stages.spawn(in_weights(layer, ("wout", layer - 1)))
         stages.spawn(next_gather(layer))
         if layer < last:
             stages.spawn(forward_sum(layer))
-        stages.spawn(out_weights(layer, ("win sent", layer), later=3))
+        stages.spawn(out_weights(layer, ("win sent", layer)))
     stages.spawn(last_gradient(("normed sent", last)))
     for layer in reversed(range(LAYERS)):
         stages.spawn(backward_sum(layer))
         if layer > 0:
             stages.spawn(next_gradient(layer))
-    stages.spawn(forward_sum(last, ("grad sent", last)))
+    stages.spawn(forward_sum(last, ("normed sent", last)))
     for layer in reversed(range(LAYERS)):
-        stages.spawn(out_grads(layer, ("grad gathered", layer)))
-        stages.spawn(in_grads(layer))
-        stages.spawn(all_grads(layer, *([] if layer == last else [("final in", layer + 1)])))
+        stages.spawn(rest_grads(layer, ("gin", layer, 0 if layer else 1)))
+        stages.spawn(qkv_grads(layer))
+        stages.spawn(final_qkv(layer, *([] if layer == last else [("final qkv", layer + 1)])))
+        stages.spawn(final_rest(layer, *([] if layer == last else [("final rest", layer + 1)])))
     stages.spawn(
         all_rows(
-            ("hidden", LAYERS), lambda: (box["hidden", LAYERS] * own_valid).astype(BF16), "block out"
+            ("hidden", LAYERS), lambda: rows_out(own_at, box["hidden", LAYERS], S, C), "block out"
         )
     )
-    stages.spawn(all_rows(("grad", 0), lambda: box["grad low", 0], "grad input"))
+    stages.spawn(all_rows(("grad", 0), lambda: rows_out(own_at, box["grad low", 0], S, C), "grad input"))
     stages.spawn(all_sums(("grad", 0)))
     stages.run()
 
     small, part = box["sums"]
-    small = from_held(small.reshape(LAYERS, 3, width))
+    small = small.reshape(LAYERS, 3, width)
     part = part.reshape(LAYERS, 3 * nt + ft)
-    grad_qkv, grad_up = box["final in", 0]
-    grad_out, grad_down = box["final out", 0]
+    (grad_qkv,) = box["final qkv", 0]
+    grad_out, grad_down, grad_up = box["final rest", 0]
     return (
         box["block out"],
         box["grad input"],

time: 1040 us -> 949 us (0.912)
  local copies, waits for them, and re-layouts: 206 us -> 87.5 us
  starting transfers between devices: 208 us -> 233 us
  other arithmetic: 50.4 us -> 29.4 us
  waiting for transfers between devices: 334 us -> 350 us
    unnamed x860 -> x630, local copies, waits for them, and re-layouts: 140 us -> 72.1 us
    reshape x15 -> x4, local copies, waits for them, and re-layouts: 23.1 us -> 2.67 us  [the longest x2 2.63 us: piece(): return lax.dynamic_slice(grad, at, (1, 1, d, wide)).reshape(d, wide)]
    ppermute x98 -> x99, waiting for transfers between devices: 24.8 us -> 44.2 us  [swap(): return lax.ppermute(block, 'tp', [(i, i ^ bit) for i in range(self.T)])]
    ppermute x43 -> x51, starting transfers between devices: 71.4 us -> 84.6 us  [shift(): return lax.ppermute(block, 'slot', [(i, (i + k) % S) for i in range(S)])]
    ppermute x8, waiting for transfers between devices: 19.4 us -> 6.27 us  [ctx_before(): lax.ppermute(block, 'ctx', [(i, i + j) for i in range(C - j)])[None]]
    ppermute x8 -> x19, starting transfers between devices: 11.4 us -> 23.5 us  [ctx_others(): lax.ppermute(block, 'ctx', [(i, (i + j) % C) for i in range(C)])]
    ppermute x8 -> x19, waiting for transfers between devices: 11.4 us -> 23.3 us  [ctx_others(): lax.ppermute(block, 'ctx', [(i, (i + j) % C) for i in range(C)])]
    convert_element_type x12, other arithmetic: 19 us -> 7.77 us  [total(): sum((a.astype(F32) for a in more), sum((a.astype(F32) for a in far[k])))]
  transfers between devices with their start and end apart: 190 -> 211, of which waited for: 46 -> 58; matrix products, arithmetic and copies ran while one was open for 11% -> 5% of each run, Pallas kernels for 20% -> 22%
where the time goes in v2:
time: 949 us; the launch traced here: 940 us
  waiting for transfers between devices  350 us (37%)
  starting transfers between devices  233 us (25%)
  Pallas kernels  220 us (23%)
  local copies, waits for them, and re-layouts  87.5 us (9%)
  other arithmetic  29.4 us (3%)
  between operations  19.9 us (2%)
    ppermute x51, waiting for transfers between devices, shift(): return lax.ppermute(block, 'slot', [(i, (i + k) % S) for i in range(S)])  208 us
    ppermute x51, starting transfers between devices, shift(): return lax.ppermute(block, 'slot', [(i, (i + k) % S) for i in range(S)])  84.6 us
    unnamed x630, local copies, waits for them, and re-layouts  72.1 us
    pallas_call x4, Pallas kernels, weight_grad(): pl.pallas_call(functools.partial(weight_grad_kernel, tuple(counts)), grid...  48.5 us
    ppermute x99, starting transfers between devices, swap(): return lax.ppermute(block, 'tp', [(i, i ^ bit) for i in range(self.T)])  45.8 us
    ppermute x99, waiting for transfers between devices, swap(): return lax.ppermute(block, 'tp', [(i, i ^ bit) for i in range(self.T)])  44.2 us
    ppermute x8, waiting for transfers between devices, ctx_return(): lax.ppermute(blocks[j - 1], 'ctx', [(i, i - j) for i in range(j, C)])[None]  32 us
    ppermute x8, starting transfers between devices, ctx_before(): lax.ppermute(block, 'ctx', [(i, i + j) for i in range(C - j)])[None]  28.8 us
  transfers between devices with their start and end apart: 211, of which 58 were waited for; matrix products, arithmetic and copies ran while one was open for 5% of the time, Pallas kernels for 22%

profile of v2, /device:TPU:0, one launch (start us, length us, event | category | flops | bytes accessed | tf_op | source)
XLA Modules:
  0.0 940.4 jit_solution(11703747260906182520)
XLA Ops:
  23.6 16.8 %collective-permute-done.5 = s32[1]{0:T(128)} collective-permute-done((s32[1]{0:T(128)}, s32[1]{0:T(128)}, u32[]{:S(2)}, u32[]{:S(2)}) %collective-permute-start.5) | collective-permute-done | bytes 36 | tf_op jit(solution)/shard_map/ppermute | solution.py:819
  49.8 13.6 %collective-permute-done.6.refs_6_ = bf16[256,896]{1,0:T(8,128)(2,1)} collective-permute-done((bf16[256,896]{1,0:T(8,128)(2,1)}, bf16[256,896]{1,0:T(8,128)(2,1)}, u32[]{:S(2)}, u32[]{:S(2)}) %collective-permute-start.6) | collective-permute-done | bytes 458784 | tf_op jit(solution)/shard_map/ppermute | solution.py:819
  72.6 8.8 collective-permute-done.9.refs_7_
  137.6 15.3 %collective-permute-done.25.refs_6_ = bf16[256,640]{1,0:T(8,128)(2,1)S(1)} collective-permute-done((bf16[256,640]{1,0:T(8,128)(2,1)S(1)}, bf16[256,640]{1,0:T(8,128)(2,1)S(1)}, u32[]{:S(2)}, u32[]{:S(2)}) %collective-permute-start.25) | collective-permute-done | bytes 327712 | tf_op jit(solution)/shard_map/ppermute | solution.py:819
  224.9 11.3 %collective-permute-done.47.refs_6_ = bf16[128,896]{1,0:T(8,128)(2,1)S(1)} collective-permute-done((bf16[128,896]{1,0:T(8,128)(2,1)S(1)}, bf16[128,896]{1,0:T(8,128)(2,1)S(1)}, u32[]{:S(2)}, u32[]{:S(2)}) %collective-permute-start.47) | collective-permute-done | bytes 229408 | tf_op jit(solution)/shard_map/ppermute | solution.py:819
  244.1 21.0 %collective-permute-done.54.refs_8_ = bf16[128,896]{1,0:T(8,128)(2,1)S(1)} collective-permute-done((bf16[128,896]{1,0:T(8,128)(2,1)S(1)}, bf16[128,896]{1,0:T(8,128)(2,1)S(1)}, u32[]{:S(2)}, u32[]{:S(2)}) %collective-permute-start.54) | collective-permute-done | bytes 229408 | tf_op jit(solution)/shard_map/ppermute | solution.py:819
  275.2 10.6 %collective-permute-done.59.refs_2_ = bf16[256,640]{1,0:T(8,128)(2,1)S(1)} collective-permute-done((bf16[256,640]{1,0:T(8,128)(2,1)S(1)}, bf16[256,640]{1,0:T(8,128)(2,1)S(1)}, u32[]{:S(2)}, u32[]{:S(2)}) %collective-permute-start.59) | collective-permute-done | bytes 327712 | tf_op jit(solution)/shard_map/ppermute | solution.py:819
  291.9 14.7 %collective-permute-done.61.refs_4_ = bf16[256,640]{1,0:T(8,128)(2,1)S(1)} collective-permute-done((bf16[256,640]{1,0:T(8,128)(2,1)S(1)}, bf16[256,640]{1,0:T(8,128)(2,1)S(1)}, u32[]{:S(2)}, u32[]{:S(2)}) %collective-permute-start.61) | collective-permute-done | bytes 327712 | tf_op jit(solution)/shard_map/ppermute | solution.py:819
  442.8 8.0 collective-permute-done.104
  478.5 16.3 %weight_grad.4 = bf16[2048,1152]{1,0:T(8,128)(2,1)S(1)} custom-call(bf16[128,2048]{1,0:T(8,128)(2,1)S(1)} %get-tuple-element.998.refs_0_, bf16[128,2048]{1,0:T(8,128)(2,1)S(1)} %get-tuple-element.1010.refs_1_, bf16[128,2048]{1,0:T(8,128)(2,1)S(1)} %get-tuple-element.1011.refs_2_, bf16[128,2048]{1,0:T(8,128)(2,1)S(1)} %get-tuple-element.1012.refs_3_, ...), custom_call_target="tpu_custom_call" | custom-call | flops 14495514624 | bytes 13107200 | tf_op jit(solution)/shard_map/weight_grad/pallas_call | solution.py:490
  509.8 12.0 %collective-permute-done.118 = bf16[512,256]{1,0:T(8,128)(2,1)S(1)} collective-permute-done((bf16[512,256]{1,0:T(8,128)(2,1)S(1)}, bf16[512,256]{1,0:T(8,128)(2,1)S(1)}, u32[]{:S(2)}, u32[]{:S(2)}) %collective-permute-start.118) | collective-permute-done | bytes 262176 | tf_op jit(solution)/shard_map/ppermute | solution.py:924
  547.2 9.0 collective-permute-done.123
  579.3 9.3 collective-permute-done.131.refs_1_
  594.3 8.1 weight_grad.5
  606.8 9.4 collective-permute-done.140.refs_2_
  739.2 15.8 %weight_grad.6 = bf16[2048,1152]{1,0:T(8,128)(2,1)S(1)} custom-call(bf16[128,2048]{1,0:T(8,128)(2,1)} %get-tuple-element.1228.refs_0_, bf16[128,2048]{1,0:T(8,128)(2,1)S(1)} %copy-done.131, bf16[128,2048]{1,0:T(8,128)(2,1)S(1)} %copy-done.134, bf16[128,2048]{1,0:T(8,128)(2,1)} %collective-permute-done.149.refs_3_, bf16[128,2048]{1,0:T(8,128)(2,1)S(1)} %copy-done.129, ...), custom_call_target="tpu_custom_call" | custom-call | flops 14495514624 | bytes 13107200 | tf_op jit(solution)/shard_map/weight_grad/pallas_call | solution.py:490
  763.3 7.6 collective-permute-done.168
  782.2 8.3 weight_grad.7
  790.6 8.7 collective-permute-done.179
  815.5 13.8 %collective-permute-done.184 = bf16[128,1152]{1,0:T(8,128)(2,1)S(1)} collective-permute-done((bf16[128,1152]{1,0:T(8,128)(2,1)S(1)}, bf16[128,1152]{1,0:T(8,128)(2,1)S(1)}, u32[]{:S(2)}, u32[]{:S(2)}) %collective-permute-start.184) | collective-permute-done | bytes 294944 | tf_op jit(solution)/shard_map/ppermute | solution.py:819
  848.8 8.9 collective-permute-done.188
  870.2 14.4 %collective-permute-done.199 = f32[19456]{0:T(1024)S(1)} collective-permute-done((f32[19456]{0:T(1024)S(1)}, f32[19456]{0:T(1024)S(1)}, u32[]{:S(2)}, u32[]{:S(2)}) %collective-permute-start.199) | collective-permute-done | bytes 77856 | tf_op jit(solution)/shard_map/ppermute | solution.py:819
  894.1 8.6 collective-permute-done.193.refs_2_
  914.8 8.2 collective-permute-done.204.refs_3_
  (1220 shorter events, 641.9 us)
Async XLA Ops:
  7.2 664.4 %reduce-scatter.3.cloned.1.call-start = ((), (), s32[]{:S(2)}) async-start(), calls=%async_computation.2 | async-start | bytes 7077888 | tf_op jit(solution)/shard_map/reduce_scatter | solution.py:985
  210.9 25.8 %collective-permute-start.41 = (bf16[128,2048]{1,0:T(8,128)(2,1)S(1)}, bf16[128,2048]{1,0:T(8,128)(2,1)S(1)}, u32[]{:S(2)}, u32[]{:S(2)}) collective-permute-start(bf16[128,2048]{1,0:T(8,128)(2,1)S(1)} %add_convert_fusion.30), channel_id=1, source_target_pairs={{16,8},{24,16},{17,9},{25,17},{18,10},{26,18},{19,11},{27,19},{20,... | collective-permute-start | bytes 1572872 | tf_op jit(solution)/shard_map/ppermute | solution.py:891
  236.9 28.2 %collective-permute-start.49 = (bf16[128,2048]{1,0:T(8,128)(2,1)S(1)}, bf16[128,2048]{1,0:T(8,128)(2,1)S(1)}, u32[]{:S(2)}, u32[]{:S(2)}) collective-permute-start(bf16[128,2048]{1,0:T(8,128)(2,1)S(1)} %add_convert_fusion.28), channel_id=1, source_target_pairs={{0,2},{1,3},{2,0},{3,1},{4,6},{5,7},{6,4},{7,5},{8,10},{9,11},{10,... | collective-permute-start | bytes 1572872 | tf_op jit(solution)/shard_map/ppermute | solution.py:815
  238.8 26.3 %collective-permute-start.50 = (bf16[128,2048]{1,0:T(8,128)(2,1)S(1)}, bf16[128,2048]{1,0:T(8,128)(2,1)S(1)}, u32[]{:S(2)}, u32[]{:S(2)}) collective-permute-start(bf16[128,2048]{1,0:T(8,128)(2,1)S(1)} %add_convert_fusion.27), channel_id=1, source_target_pairs={{0,8},{8,16},{16,24},{24,0},{1,9},{9,17},{17,25},{25,1},{2,10},{10... | collective-permute-start | bytes 1572872 | tf_op jit(solution)/shard_map/ppermute | solution.py:819
  381.0 34.7 %collective-permute-start.88 = (bf16[128,2048]{1,0:T(8,128)(2,1)S(1)}, bf16[128,2048]{1,0:T(8,128)(2,1)S(1)}, u32[]{:S(2)}, u32[]{:S(2)}) collective-permute-start(bf16[128,2048]{1,0:T(8,128)(2,1)S(1)} %collective-permute-done.82.refs_0_.refs_4_), channel_id=1, source_target_pairs={{8,0},{16,8},{9,1},{17,9},{10,2},{18,10},{11,3},{19,11},{12,4},{20... | collective-permute-start | bytes 1572872 | tf_op jit(solution)/shard_map/ppermute | solution.py:852
  497.1 187.7 %reduce-scatter.5.cloned.1.call-start = ((), (), s32[]{:S(2)}) async-start(), calls=%async_computation.3 | async-start | bytes 2359296 | tf_op jit(solution)/shard_map/reduce_scatter | solution.py:985
  503.5 25.6 %collective-permute-start.117 = (bf16[128,2048]{1,0:T(8,128)(2,1)S(1)}, bf16[128,2048]{1,0:T(8,128)(2,1)S(1)}, u32[]{:S(2)}, u32[]{:S(2)}) collective-permute-start(bf16[128,2048]{1,0:T(8,128)(2,1)S(1)} %get-tuple-element.1132), channel_id=1, source_target_pairs={{0,1},{1,0},{2,3},{3,2},{4,5},{5,4},{6,7},{7,6},{8,9},{9,8},{10,11... | collective-permute-start | bytes 1572872 | tf_op jit(solution)/shard_map/ppermute | solution.py:815
  572.5 29.9 %collective-permute-start.137 = (bf16[128,2048]{1,0:T(8,128)(2,1)S(1)}, bf16[128,2048]{1,0:T(8,128)(2,1)S(1)}, u32[]{:S(2)}, u32[]{:S(2)}) collective-permute-start(bf16[128,2048]{1,0:T(8,128)(2,1)S(1)} %get-tuple-element.1204), channel_id=1, source_target_pairs={{0,1},{1,0},{2,3},{3,2},{4,5},{5,4},{6,7},{7,6},{8,9},{9,8},{10,11... | collective-permute-start | bytes 1572872 | tf_op jit(solution)/shard_map/ppermute | solution.py:815
  666.4 33.6 %collective-permute-start.133 = (bf16[128,2048]{1,0:T(8,128)(2,1)}, bf16[128,2048]{1,0:T(8,128)(2,1)}, u32[]{:S(2)}, u32[]{:S(2)}) collective-permute-start(bf16[128,2048]{1,0:T(8,128)(2,1)} %collective-permute-done.131.refs_1_), channel_id=1, source_target_pairs={{0,1},{1,0},{2,3},{3,2},{4,5},{5,4},{6,7},{7,6},{8,9},{9,8},{10,11... | collective-permute-start | bytes 1572872 | tf_op jit(solution)/shard_map/ppermute | solution.py:815
  669.3 29.7 %collective-permute-start.155 = (bf16[128,2048]{1,0:T(8,128)(2,1)}, bf16[128,2048]{1,0:T(8,128)(2,1)}, u32[]{:S(2)}, u32[]{:S(2)}) collective-permute-start(bf16[128,2048]{1,0:T(8,128)(2,1)} %broadcast_select_fusion.refs_0_.refs_8_), channel_id=1, source_target_pairs={{0,2},{1,3},{2,0},{3,1},{4,6},{5,7},{6,4},{7,5},{8,10},{9,11},{10,... | collective-permute-start | bytes 1572872 | tf_op jit(solution)/shard_map/ppermute | solution.py:815
  670.2 28.8 %collective-permute-start.156 = (bf16[128,2048]{1,0:T(8,128)(2,1)}, bf16[128,2048]{1,0:T(8,128)(2,1)}, u32[]{:S(2)}, u32[]{:S(2)}) collective-permute-start(bf16[128,2048]{1,0:T(8,128)(2,1)} %broadcast_select_fusion.refs_0_.refs_8_), channel_id=1, source_target_pairs={{0,1},{1,0},{2,3},{3,2},{4,5},{5,4},{6,7},{7,6},{8,9},{9,8},{10,11... | collective-permute-start | bytes 1572872 | tf_op jit(solution)/shard_map/ppermute | solution.py:815
  708.5 46.5 %collective-permute-start.164 = (bf16[128,384]{1,0:T(8,128)(2,1)S(1)}, bf16[128,384]{1,0:T(8,128)(2,1)S(1)}, u32[]{:S(2)}, u32[]{:S(2)}) collective-permute-start(bf16[128,384]{1,0:T(8,128)(2,1)S(1)} %get-tuple-element.1482), channel_id=1, source_target_pairs={{0,16},{8,24},{16,0},{24,8},{1,17},{9,25},{17,1},{25,9},{2,18},{10... | collective-permute-start | bytes 294920 | tf_op jit(solution)/shard_map/ppermute | solution.py:819
  723.0 40.2 %collective-permute-start.169 = (bf16[128,384]{1,0:T(8,128)(2,1)S(1)}, bf16[128,384]{1,0:T(8,128)(2,1)S(1)}, u32[]{:S(2)}, u32[]{:S(2)}) collective-permute-start(bf16[128,384]{1,0:T(8,128)(2,1)S(1)} %get-tuple-element.1481), channel_id=1, source_target_pairs={{0,16},{8,24},{16,0},{24,8},{1,17},{9,25},{17,1},{25,9},{2,18},{10... | collective-permute-start | bytes 294920 | tf_op jit(solution)/shard_map/ppermute | solution.py:819
  727.8 29.9 %collective-permute-start.163 = (bf16[128,1152]{1,0:T(8,128)(2,1)S(1)}, bf16[128,1152]{1,0:T(8,128)(2,1)S(1)}, u32[]{:S(2)}, u32[]{:S(2)}) collective-permute-start(bf16[128,1152]{1,0:T(8,128)(2,1)S(1)} %get-tuple-element.1469), channel_id=1, source_target_pairs={{0,16},{8,24},{16,0},{24,8},{1,17},{9,25},{17,1},{25,9},{2,18},{10... | collective-permute-start | bytes 884744 | tf_op jit(solution)/shard_map/ppermute | solution.py:819
  771.1 28.2 %collective-permute-start.179 = (bf16[256,1152]{1,0:T(8,128)(2,1)S(1)}, bf16[256,1152]{1,0:T(8,128)(2,1)S(1)}, u32[]{:S(2)}, u32[]{:S(2)}) collective-permute-start(bf16[256,1152]{1,0:T(8,128)(2,1)S(1)} %get-tuple-element.1464), channel_id=1, source_target_pairs={{0,4},{4,0},{1,5},{5,1},{2,6},{6,2},{3,7},{7,3},{8,12},{12,8},{9,1... | collective-permute-start | bytes 1769480 | tf_op jit(solution)/shard_map/ppermute | solution.py:1008
  773.3 26.0 %collective-permute-start.173 = (bf16[128,2048]{1,0:T(8,128)(2,1)S(1)}, bf16[128,2048]{1,0:T(8,128)(2,1)S(1)}, u32[]{:S(2)}, u32[]{:S(2)}) collective-permute-start(bf16[128,2048]{1,0:T(8,128)(2,1)S(1)} %add_convert_fusion.9), channel_id=1, source_target_pairs={{16,8},{24,16},{17,9},{25,17},{18,10},{26,18},{19,11},{27,19},{20,... | collective-permute-start | bytes 1572872 | tf_op jit(solution)/shard_map/ppermute | solution.py:891
  799.8 29.5 %collective-permute-start.180 = (bf16[128,2048]{1,0:T(8,128)(2,1)S(1)}, bf16[128,2048]{1,0:T(8,128)(2,1)S(1)}, u32[]{:S(2)}, u32[]{:S(2)}) collective-permute-start(bf16[128,2048]{1,0:T(8,128)(2,1)S(1)} %add_convert_fusion.7), channel_id=1, source_target_pairs={{0,2},{1,3},{2,0},{3,1},{4,6},{5,7},{6,4},{7,5},{8,10},{9,11},{10,... | collective-permute-start | bytes 1572872 | tf_op jit(solution)/shard_map/ppermute | solution.py:815
  801.1 28.2 %collective-permute-start.181 = (bf16[128,2048]{1,0:T(8,128)(2,1)S(1)}, bf16[128,2048]{1,0:T(8,128)(2,1)S(1)}, u32[]{:S(2)}, u32[]{:S(2)}) collective-permute-start(bf16[128,2048]{1,0:T(8,128)(2,1)S(1)} %add_convert_fusion.6), channel_id=1, source_target_pairs={{0,8},{8,16},{16,24},{24,0},{1,9},{9,17},{17,25},{25,1},{2,10},{10... | collective-permute-start | bytes 1572872 | tf_op jit(solution)/shard_map/ppermute | solution.py:819
  802.7 26.6 %collective-permute-start.184 = (bf16[128,1152]{1,0:T(8,128)(2,1)S(1)}, bf16[128,1152]{1,0:T(8,128)(2,1)S(1)}, u32[]{:S(2)}, u32[]{:S(2)}) collective-permute-start(bf16[128,1152]{1,0:T(8,128)(2,1)S(1)} %get-tuple-element.1487), channel_id=1, source_target_pairs={{0,16},{8,24},{16,0},{24,8},{1,17},{9,25},{17,1},{25,9},{2,18},{10... | collective-permute-start | bytes 884744 | tf_op jit(solution)/shard_map/ppermute | solution.py:819
  806.3 30.3 %collective-permute-start.189 = (bf16[256,1152]{1,0:T(8,128)(2,1)S(1)}, bf16[256,1152]{1,0:T(8,128)(2,1)}, u32[]{:S(2)}, u32[]{:S(2)}) collective-permute-start(bf16[256,1152]{1,0:T(8,128)(2,1)S(1)} %get-tuple-element.1460), channel_id=1, source_target_pairs={{0,4},{4,0},{1,5},{5,1},{2,6},{6,2},{3,7},{7,3},{8,12},{12,8},{9,1... | collective-permute-start | bytes 1769480 | tf_op jit(solution)/shard_map/ppermute | solution.py:1008
  831.2 26.6 %collective-permute-start.186 = (bf16[128,2048]{1,0:T(8,128)(2,1)}, bf16[128,2048]{1,0:T(8,128)(2,1)}, u32[]{:S(2)}, u32[]{:S(2)}) collective-permute-start(bf16[128,2048]{1,0:T(8,128)(2,1)} %add_convert_fusion.5), channel_id=1, source_target_pairs={{0,2},{1,3},{2,0},{3,1},{4,6},{5,7},{6,4},{7,5},{8,10},{9,11},{10,... | collective-permute-start | bytes 1572872 | tf_op jit(solution)/shard_map/ppermute | solution.py:815
  862.2 40.5 %collective-permute-start.197 = (bf16[128,2048]{1,0:T(8,128)(2,1)S(1)}, bf16[128,2048]{1,0:T(8,128)(2,1)}, u32[]{:S(2)}, u32[]{:S(2)}) collective-permute-start(bf16[128,2048]{1,0:T(8,128)(2,1)S(1)} %rows_out.3.refs_0_), channel_id=1, source_target_pairs={{0,2},{1,3},{2,0},{3,1},{4,6},{5,7},{6,4},{7,5},{8,10},{9,11},{10,... | collective-permute-start | bytes 1572872 | tf_op jit(solution)/shard_map/ppermute | solution.py:815
  863.1 39.6 %collective-permute-start.198 = (bf16[128,2048]{1,0:T(8,128)(2,1)S(1)}, bf16[128,2048]{1,0:T(8,128)(2,1)}, u32[]{:S(2)}, u32[]{:S(2)}) collective-permute-start(bf16[128,2048]{1,0:T(8,128)(2,1)S(1)} %rows_out.3.refs_0_), channel_id=1, source_target_pairs={{0,1},{1,0},{2,3},{3,2},{4,5},{5,4},{6,7},{7,6},{8,9},{9,8},{10,11... | collective-permute-start | bytes 1572872 | tf_op jit(solution)/shard_map/ppermute | solution.py:815
  864.1 38.6 %collective-permute-start.192 = (bf16[256,1152]{1,0:T(8,128)(2,1)}, bf16[256,1152]{1,0:T(8,128)(2,1)S(1)}, u32[]{:S(2)}, u32[]{:S(2)}) collective-permute-start(bf16[256,1152]{1,0:T(8,128)(2,1)} %add_convert_fusion.2), channel_id=1, source_target_pairs={{0,8},{8,16},{16,24},{24,0},{1,9},{9,17},{17,25},{25,1},{2,10},{10... | collective-permute-start | bytes 1769480 | tf_op jit(solution)/shard_map/ppermute | solution.py:819
  (500 other events, 9158.7 us)
Sparse Core Ops, SparseCore 0:
  497.2 66.1 reduce-scatter.2
  633.7 24.4 reduce-scatter.4

commit v3 on v2

--- a/solution.py
+++ b/solution.py
@@ -1333,7 +1333,7 @@
     stages.spawn(forward_sum(0))
     stages.spawn(out_weights(0, ("normed sent", 0)))
     for layer in range(1, LAYERS):
-        stages.spawn(in_weights(layer, ("wout", layer - 1)))
+        stages.spawn(in_weights(layer, ("wout sent", layer - 1)))
         stages.spawn(next_gather(layer))
         if layer < last:
             stages.spawn(forward_sum(layer))

time: 949 us -> 940 us (level)
  waiting for transfers between devices: 350 us -> 338 us
  transfers between devices with their start and end apart: 211 -> 211, of which waited for: 58 -> 54; matrix products, arithmetic and copies ran while one was open for 5% -> 5% of each run, Pallas kernels for 22% -> 22%
where the time goes in v3:
time: 940 us; the launch traced here: 933 us
  waiting for transfers between devices  338 us (36%)
  starting transfers between devices  238 us (25%)
  Pallas kernels  220 us (23%)
  local copies, waits for them, and re-layouts  87.5 us (9%)
  other arithmetic  29 us (3%)
  between operations  19.9 us (2%)
    ppermute x51, waiting for transfers between devices, shift(): return lax.ppermute(block, 'slot', [(i, (i + k) % S) for i in range(S)])  202 us
    ppermute x51, starting transfers between devices, shift(): return lax.ppermute(block, 'slot', [(i, (i + k) % S) for i in range(S)])  88.2 us
    unnamed x630, local copies, waits for them, and re-layouts  72.1 us
    ppermute x99, starting transfers between devices, swap(): return lax.ppermute(block, 'tp', [(i, i ^ bit) for i in range(self.T)])  48.5 us
    pallas_call x4, Pallas kernels, weight_grad(): pl.pallas_call(functools.partial(weight_grad_kernel, tuple(counts)), grid...  48.5 us
    ppermute x99, waiting for transfers between devices, swap(): return lax.ppermute(block, 'tp', [(i, i ^ bit) for i in range(self.T)])  38.4 us
    ppermute x8, waiting for transfers between devices, add(): lax.ppermute(piece(k, j), 'ctx', [(i, (i + j) % C) for i in range(C)])  27.8 us
    pallas_call x8, Pallas kernels, attend_back(): pl.pallas_call(functools.partial(attend_back_kernel, rows_each), grid=(ru...  27.5 us
  transfers between devices with their start and end apart: 211, of which 54 were waited for; matrix products, arithmetic and copies ran while one was open for 5% of the time, Pallas kernels for 22%

profile of v3, /device:TPU:0, one launch (start us, length us, event | category | flops | bytes accessed | tf_op | source)
XLA Modules:
  0.0 932.7 jit_solution(18187300989695367552)
XLA Ops:
  23.6 16.8 %collective-permute-done.5 = s32[1]{0:T(128)} collective-permute-done((s32[1]{0:T(128)}, s32[1]{0:T(128)}, u32[]{:S(2)}, u32[]{:S(2)}) %collective-permute-start.5) | collective-permute-done | bytes 36 | tf_op jit(solution)/shard_map/ppermute | solution.py:819
  49.8 13.6 %collective-permute-done.6.refs_6_ = bf16[256,896]{1,0:T(8,128)(2,1)} collective-permute-done((bf16[256,896]{1,0:T(8,128)(2,1)}, bf16[256,896]{1,0:T(8,128)(2,1)}, u32[]{:S(2)}, u32[]{:S(2)}) %collective-permute-start.6) | collective-permute-done | bytes 458784 | tf_op jit(solution)/shard_map/ppermute | solution.py:819
  72.6 8.8 collective-permute-done.9.refs_7_
  137.8 15.1 %collective-permute-done.25.refs_6_ = bf16[256,640]{1,0:T(8,128)(2,1)S(1)} collective-permute-done((bf16[256,640]{1,0:T(8,128)(2,1)S(1)}, bf16[256,640]{1,0:T(8,128)(2,1)S(1)}, u32[]{:S(2)}, u32[]{:S(2)}) %collective-permute-start.25) | collective-permute-done | bytes 327712 | tf_op jit(solution)/shard_map/ppermute | solution.py:819
  239.7 10.4 %collective-permute-done.43.refs_8_ = bf16[128,896]{1,0:T(8,128)(2,1)S(1)} collective-permute-done((bf16[128,896]{1,0:T(8,128)(2,1)S(1)}, bf16[128,896]{1,0:T(8,128)(2,1)S(1)}, u32[]{:S(2)}, u32[]{:S(2)}) %collective-permute-start.43) | collective-permute-done | bytes 229408 | tf_op jit(solution)/shard_map/ppermute | solution.py:819
  257.0 12.0 %collective-permute-done.51.refs_9_ = bf16[128,896]{1,0:T(8,128)(2,1)S(1)} collective-permute-done((bf16[128,896]{1,0:T(8,128)(2,1)S(1)}, bf16[128,896]{1,0:T(8,128)(2,1)S(1)}, u32[]{:S(2)}, u32[]{:S(2)}) %collective-permute-start.51) | collective-permute-done | bytes 229408 | tf_op jit(solution)/shard_map/ppermute | solution.py:932
  279.1 17.9 %collective-permute-done.61.refs_4_ = bf16[256,640]{1,0:T(8,128)(2,1)S(1)} collective-permute-done((bf16[256,640]{1,0:T(8,128)(2,1)S(1)}, bf16[256,640]{1,0:T(8,128)(2,1)S(1)}, u32[]{:S(2)}, u32[]{:S(2)}) %collective-permute-start.61) | collective-permute-done | bytes 327712 | tf_op jit(solution)/shard_map/ppermute | solution.py:819
  302.9 13.0 %collective-permute-done.63.refs_6_ = bf16[128,640]{1,0:T(8,128)(2,1)S(1)} collective-permute-done((bf16[128,640]{1,0:T(8,128)(2,1)S(1)}, bf16[128,640]{1,0:T(8,128)(2,1)S(1)}, u32[]{:S(2)}, u32[]{:S(2)}) %collective-permute-start.63) | collective-permute-done | bytes 163872 | tf_op jit(solution)/shard_map/ppermute | solution.py:819
  432.2 10.1 %collective-permute-done.104 = bf16[512,256]{1,0:T(8,128)(2,1)S(1)} collective-permute-done((bf16[512,256]{1,0:T(8,128)(2,1)S(1)}, bf16[512,256]{1,0:T(8,128)(2,1)S(1)}, u32[]{:S(2)}, u32[]{:S(2)}) %collective-permute-start.104) | collective-permute-done | bytes 262176 | tf_op jit(solution)/shard_map/ppermute | solution.py:924
  466.6 16.3 %weight_grad.4 = bf16[2048,1152]{1,0:T(8,128)(2,1)S(1)} custom-call(bf16[128,2048]{1,0:T(8,128)(2,1)S(1)} %get-tuple-element.998.refs_0_, bf16[128,2048]{1,0:T(8,128)(2,1)S(1)} %get-tuple-element.1008.refs_1_, bf16[128,2048]{1,0:T(8,128)(2,1)S(1)} %get-tuple-element.1009.refs_2_, bf16[128,2048]{1,0:T(8,128)(2,1)S(1)} %get-tuple-element.1010.refs_3_, ...), custom_call_target="tpu_custom_call" | custom-call | flops 14495514624 | bytes 13107200 | tf_op jit(solution)/shard_map/weight_grad/pallas_call | solution.py:490
  500.5 9.4 %collective-permute-done.118 = bf16[512,256]{1,0:T(8,128)(2,1)S(1)} collective-permute-done((bf16[512,256]{1,0:T(8,128)(2,1)S(1)}, bf16[512,256]{1,0:T(8,128)(2,1)S(1)}, u32[]{:S(2)}, u32[]{:S(2)}) %collective-permute-start.118) | collective-permute-done | bytes 262176 | tf_op jit(solution)/shard_map/ppermute | solution.py:924
  546.4 7.5 collective-permute-start.130
  570.0 9.3 collective-permute-done.131.refs_1_
  585.2 8.1 weight_grad.5
  598.0 9.3 collective-permute-done.140.refs_2_
  726.7 15.8 %weight_grad.6 = bf16[2048,1152]{1,0:T(8,128)(2,1)S(1)} custom-call(bf16[128,2048]{1,0:T(8,128)(2,1)} %get-tuple-element.1228.refs_0_, bf16[128,2048]{1,0:T(8,128)(2,1)S(1)} %copy-done.131, bf16[128,2048]{1,0:T(8,128)(2,1)S(1)} %copy-done.134, bf16[128,2048]{1,0:T(8,128)(2,1)} %collective-permute-done.149.refs_3_, bf16[128,2048]{1,0:T(8,128)(2,1)S(1)} %copy-done.129, ...), custom_call_target="tpu_custom_call" | custom-call | flops 14495514624 | bytes 13107200 | tf_op jit(solution)/shard_map/weight_grad/pallas_call | solution.py:490
  770.7 8.3 weight_grad.7
  779.1 11.0 %collective-permute-done.179 = bf16[256,1152]{1,0:T(8,128)(2,1)S(1)} collective-permute-done((bf16[256,1152]{1,0:T(8,128)(2,1)S(1)}, bf16[256,1152]{1,0:T(8,128)(2,1)S(1)}, u32[]{:S(2)}, u32[]{:S(2)}) %collective-permute-start.179) | collective-permute-done | bytes 589856 | tf_op jit(solution)/shard_map/ppermute | solution.py:1008
  796.7 9.6 %collective-permute-done.185 = bf16[256,1152]{1,0:T(8,128)(2,1)S(1)} collective-permute-done((bf16[256,1152]{1,0:T(8,128)(2,1)S(1)}, bf16[256,1152]{1,0:T(8,128)(2,1)S(1)}, u32[]{:S(2)}, u32[]{:S(2)}) %collective-permute-start.185) | collective-permute-done | bytes 589856 | tf_op jit(solution)/shard_map/ppermute | solution.py:1008
  806.3 15.4 %collective-permute-done.184 = bf16[128,1152]{1,0:T(8,128)(2,1)S(1)} collective-permute-done((bf16[128,1152]{1,0:T(8,128)(2,1)S(1)}, bf16[128,1152]{1,0:T(8,128)(2,1)S(1)}, u32[]{:S(2)}, u32[]{:S(2)}) %collective-permute-start.184) | collective-permute-done | bytes 294944 | tf_op jit(solution)/shard_map/ppermute | solution.py:819
  839.6 10.4 %collective-permute-done.188 = bf16[128,1152]{1,0:T(8,128)(2,1)} collective-permute-done((bf16[128,1152]{1,0:T(8,128)(2,1)}, bf16[128,1152]{1,0:T(8,128)(2,1)}, u32[]{:S(2)}, u32[]{:S(2)}) %collective-permute-start.188) | collective-permute-done | bytes 294944 | tf_op jit(solution)/shard_map/ppermute | solution.py:819
  862.5 14.4 %collective-permute-done.199 = f32[19456]{0:T(1024)S(1)} collective-permute-done((f32[19456]{0:T(1024)S(1)}, f32[19456]{0:T(1024)S(1)}, u32[]{:S(2)}, u32[]{:S(2)}) %collective-permute-start.199) | collective-permute-done | bytes 77856 | tf_op jit(solution)/shard_map/ppermute | solution.py:819
  886.5 8.6 collective-permute-done.193.refs_2_
  905.7 9.6 %collective-permute-done.204.refs_3_ = bf16[256,384]{1,0:T(8,128)(2,1)S(1)} collective-permute-done((bf16[256,384]{1,0:T(8,128)(2,1)S(1)}, bf16[256,384]{1,0:T(8,128)(2,1)S(1)}, u32[]{:S(2)}, u32[]{:S(2)}) %collective-permute-start.204) | collective-permute-done | bytes 196640 | tf_op jit(solution)/shard_map/ppermute | solution.py:819
  (1220 shorter events, 632.3 us)
Async XLA Ops:
  7.2 655.6 %reduce-scatter.3.cloned.1.call-start = ((), (), s32[]{:S(2)}) async-start(), calls=%async_computation.2 | async-start | bytes 7077888 | tf_op jit(solution)/shard_map/reduce_scatter | solution.py:985
  164.4 29.9 %collective-permute-start.40 = (bf16[512,256]{1,0:T(8,128)(2,1)S(1)}, bf16[512,256]{1,0:T(8,128)(2,1)S(1)}, u32[]{:S(2)}, u32[]{:S(2)}) collective-permute-start(bf16[512,256]{1,0:T(8,128)(2,1)S(1)} %get-tuple-element.858.own_ref), channel_id=1, source_target_pairs={{0,4},{1,5},{2,6},{3,7},{8,12},{9,13},{10,14},{11,15},{16,20},{17,... | collective-permute-start | bytes 786440 | tf_op jit(solution)/shard_map/ppermute | solution.py:916
  224.3 26.2 %collective-permute-start.45 = (bf16[128,2048]{1,0:T(8,128)(2,1)S(1)}, bf16[128,2048]{1,0:T(8,128)(2,1)S(1)}, u32[]{:S(2)}, u32[]{:S(2)}) collective-permute-start(bf16[128,2048]{1,0:T(8,128)(2,1)S(1)} %add_convert_fusion.30), channel_id=1, source_target_pairs={{16,8},{24,16},{17,9},{25,17},{18,10},{26,18},{19,11},{27,19},{20,... | collective-permute-start | bytes 1572872 | tf_op jit(solution)/shard_map/ppermute | solution.py:891
  485.2 190.9 %reduce-scatter.5.cloned.1.call-start = ((), (), s32[]{:S(2)}) async-start(), calls=%async_computation.3 | async-start | bytes 2359296 | tf_op jit(solution)/shard_map/reduce_scatter | solution.py:985
  491.6 25.6 %collective-permute-start.117 = (bf16[128,2048]{1,0:T(8,128)(2,1)S(1)}, bf16[128,2048]{1,0:T(8,128)(2,1)S(1)}, u32[]{:S(2)}, u32[]{:S(2)}) collective-permute-start(bf16[128,2048]{1,0:T(8,128)(2,1)S(1)} %get-tuple-element.1132), channel_id=1, source_target_pairs={{0,1},{1,0},{2,3},{3,2},{4,5},{5,4},{6,7},{7,6},{8,9},{9,8},{10,11... | collective-permute-start | bytes 1572872 | tf_op jit(solution)/shard_map/ppermute | solution.py:815
  563.2 30.1 %collective-permute-start.137 = (bf16[128,2048]{1,0:T(8,128)(2,1)S(1)}, bf16[128,2048]{1,0:T(8,128)(2,1)S(1)}, u32[]{:S(2)}, u32[]{:S(2)}) collective-permute-start(bf16[128,2048]{1,0:T(8,128)(2,1)S(1)} %get-tuple-element.1204), channel_id=1, source_target_pairs={{0,1},{1,0},{2,3},{3,2},{4,5},{5,4},{6,7},{7,6},{8,9},{9,8},{10,11... | collective-permute-start | bytes 1572872 | tf_op jit(solution)/shard_map/ppermute | solution.py:815
  657.5 33.6 %collective-permute-start.133 = (bf16[128,2048]{1,0:T(8,128)(2,1)}, bf16[128,2048]{1,0:T(8,128)(2,1)}, u32[]{:S(2)}, u32[]{:S(2)}) collective-permute-start(bf16[128,2048]{1,0:T(8,128)(2,1)} %collective-permute-done.131.refs_1_), channel_id=1, source_target_pairs={{0,1},{1,0},{2,3},{3,2},{4,5},{5,4},{6,7},{7,6},{8,9},{9,8},{10,11... | collective-permute-start | bytes 1572872 | tf_op jit(solution)/shard_map/ppermute | solution.py:815
  660.4 29.7 %collective-permute-start.155 = (bf16[128,2048]{1,0:T(8,128)(2,1)}, bf16[128,2048]{1,0:T(8,128)(2,1)}, u32[]{:S(2)}, u32[]{:S(2)}) collective-permute-start(bf16[128,2048]{1,0:T(8,128)(2,1)} %broadcast_select_fusion.refs_0_.refs_8_), channel_id=1, source_target_pairs={{0,2},{1,3},{2,0},{3,1},{4,6},{5,7},{6,4},{7,5},{8,10},{9,11},{10,... | collective-permute-start | bytes 1572872 | tf_op jit(solution)/shard_map/ppermute | solution.py:815
  661.5 28.6 %collective-permute-start.156 = (bf16[128,2048]{1,0:T(8,128)(2,1)}, bf16[128,2048]{1,0:T(8,128)(2,1)}, u32[]{:S(2)}, u32[]{:S(2)}) collective-permute-start(bf16[128,2048]{1,0:T(8,128)(2,1)} %broadcast_select_fusion.refs_0_.refs_8_), channel_id=1, source_target_pairs={{0,1},{1,0},{2,3},{3,2},{4,5},{5,4},{6,7},{7,6},{8,9},{9,8},{10,11... | collective-permute-start | bytes 1572872 | tf_op jit(solution)/shard_map/ppermute | solution.py:815
  699.7 42.8 %collective-permute-start.164 = (bf16[128,384]{1,0:T(8,128)(2,1)S(1)}, bf16[128,384]{1,0:T(8,128)(2,1)S(1)}, u32[]{:S(2)}, u32[]{:S(2)}) collective-permute-start(bf16[128,384]{1,0:T(8,128)(2,1)S(1)} %get-tuple-element.1482), channel_id=1, source_target_pairs={{0,16},{8,24},{16,0},{24,8},{1,17},{9,25},{17,1},{25,9},{2,18},{10... | collective-permute-start | bytes 294920 | tf_op jit(solution)/shard_map/ppermute | solution.py:819
  714.1 38.2 %collective-permute-start.169 = (bf16[128,384]{1,0:T(8,128)(2,1)S(1)}, bf16[128,384]{1,0:T(8,128)(2,1)S(1)}, u32[]{:S(2)}, u32[]{:S(2)}) collective-permute-start(bf16[128,384]{1,0:T(8,128)(2,1)S(1)} %get-tuple-element.1481), channel_id=1, source_target_pairs={{0,16},{8,24},{16,0},{24,8},{1,17},{9,25},{17,1},{25,9},{2,18},{10... | collective-permute-start | bytes 294920 | tf_op jit(solution)/shard_map/ppermute | solution.py:819
  719.0 27.5 %collective-permute-start.163 = (bf16[128,1152]{1,0:T(8,128)(2,1)S(1)}, bf16[128,1152]{1,0:T(8,128)(2,1)S(1)}, u32[]{:S(2)}, u32[]{:S(2)}) collective-permute-start(bf16[128,1152]{1,0:T(8,128)(2,1)S(1)} %get-tuple-element.1469), channel_id=1, source_target_pairs={{0,16},{8,24},{16,0},{24,8},{1,17},{9,25},{17,1},{25,9},{2,18},{10... | collective-permute-start | bytes 884744 | tf_op jit(solution)/shard_map/ppermute | solution.py:819
  763.5 26.6 %collective-permute-start.179 = (bf16[256,1152]{1,0:T(8,128)(2,1)S(1)}, bf16[256,1152]{1,0:T(8,128)(2,1)S(1)}, u32[]{:S(2)}, u32[]{:S(2)}) collective-permute-start(bf16[256,1152]{1,0:T(8,128)(2,1)S(1)} %get-tuple-element.1464), channel_id=1, source_target_pairs={{0,4},{4,0},{1,5},{5,1},{2,6},{6,2},{3,7},{7,3},{8,12},{12,8},{9,1... | collective-permute-start | bytes 1769480 | tf_op jit(solution)/shard_map/ppermute | solution.py:1008
  763.9 26.2 %collective-permute-start.173 = (bf16[128,2048]{1,0:T(8,128)(2,1)S(1)}, bf16[128,2048]{1,0:T(8,128)(2,1)S(1)}, u32[]{:S(2)}, u32[]{:S(2)}) collective-permute-start(bf16[128,2048]{1,0:T(8,128)(2,1)S(1)} %add_convert_fusion.9), channel_id=1, source_target_pairs={{16,8},{24,16},{17,9},{25,17},{18,10},{26,18},{19,11},{27,19},{20,... | collective-permute-start | bytes 1572872 | tf_op jit(solution)/shard_map/ppermute | solution.py:891
  764.7 27.2 %collective-permute-start.177 = (bf16[128,2048]{1,0:T(8,128)(2,1)S(1)}, bf16[128,2048]{1,0:T(8,128)(2,1)S(1)}, u32[]{:S(2)}, u32[]{:S(2)}) collective-permute-start(bf16[128,2048]{1,0:T(8,128)(2,1)S(1)} %add_convert_fusion.9), channel_id=1, source_target_pairs={{0,8},{8,16},{1,9},{9,17},{2,10},{10,18},{3,11},{11,19},{4,12},{12... | collective-permute-start | bytes 1572872 | tf_op jit(solution)/shard_map/ppermute | solution.py:890
  766.3 25.6 %collective-permute-start.174 = (bf16[128,2048]{1,0:T(8,128)(2,1)S(1)}, bf16[128,2048]{1,0:T(8,128)(2,1)S(1)}, u32[]{:S(2)}, u32[]{:S(2)}) collective-permute-start(bf16[128,2048]{1,0:T(8,128)(2,1)S(1)} %add_convert_fusion.8), channel_id=1, source_target_pairs={{0,2},{1,3},{2,0},{3,1},{4,6},{5,7},{6,4},{7,5},{8,10},{9,11},{10,... | collective-permute-start | bytes 1572872 | tf_op jit(solution)/shard_map/ppermute | solution.py:815
  792.1 29.6 %collective-permute-start.180 = (bf16[128,2048]{1,0:T(8,128)(2,1)S(1)}, bf16[128,2048]{1,0:T(8,128)(2,1)S(1)}, u32[]{:S(2)}, u32[]{:S(2)}) collective-permute-start(bf16[128,2048]{1,0:T(8,128)(2,1)S(1)} %add_convert_fusion.7), channel_id=1, source_target_pairs={{0,2},{1,3},{2,0},{3,1},{4,6},{5,7},{6,4},{7,5},{8,10},{9,11},{10,... | collective-permute-start | bytes 1572872 | tf_op jit(solution)/shard_map/ppermute | solution.py:815
  793.5 28.2 %collective-permute-start.181 = (bf16[128,2048]{1,0:T(8,128)(2,1)S(1)}, bf16[128,2048]{1,0:T(8,128)(2,1)S(1)}, u32[]{:S(2)}, u32[]{:S(2)}) collective-permute-start(bf16[128,2048]{1,0:T(8,128)(2,1)S(1)} %add_convert_fusion.6), channel_id=1, source_target_pairs={{0,8},{8,16},{16,24},{24,0},{1,9},{9,17},{17,25},{25,1},{2,10},{10... | collective-permute-start | bytes 1572872 | tf_op jit(solution)/shard_map/ppermute | solution.py:819
  794.5 27.2 %collective-permute-start.184 = (bf16[128,1152]{1,0:T(8,128)(2,1)S(1)}, bf16[128,1152]{1,0:T(8,128)(2,1)S(1)}, u32[]{:S(2)}, u32[]{:S(2)}) collective-permute-start(bf16[128,1152]{1,0:T(8,128)(2,1)S(1)} %get-tuple-element.1487), channel_id=1, source_target_pairs={{0,16},{8,24},{16,0},{24,8},{1,17},{9,25},{17,1},{25,9},{2,18},{10... | collective-permute-start | bytes 884744 | tf_op jit(solution)/shard_map/ppermute | solution.py:819
  796.3 30.9 %collective-permute-start.189 = (bf16[256,1152]{1,0:T(8,128)(2,1)S(1)}, bf16[256,1152]{1,0:T(8,128)(2,1)}, u32[]{:S(2)}, u32[]{:S(2)}) collective-permute-start(bf16[256,1152]{1,0:T(8,128)(2,1)S(1)} %get-tuple-element.1460), channel_id=1, source_target_pairs={{0,4},{4,0},{1,5},{5,1},{2,6},{6,2},{3,7},{7,3},{8,12},{12,8},{9,1... | collective-permute-start | bytes 1769480 | tf_op jit(solution)/shard_map/ppermute | solution.py:1008
  823.5 26.5 %collective-permute-start.186 = (bf16[128,2048]{1,0:T(8,128)(2,1)}, bf16[128,2048]{1,0:T(8,128)(2,1)}, u32[]{:S(2)}, u32[]{:S(2)}) collective-permute-start(bf16[128,2048]{1,0:T(8,128)(2,1)} %add_convert_fusion.5), channel_id=1, source_target_pairs={{0,2},{1,3},{2,0},{3,1},{4,6},{5,7},{6,4},{7,5},{8,10},{9,11},{10,... | collective-permute-start | bytes 1572872 | tf_op jit(solution)/shard_map/ppermute | solution.py:815
  854.4 40.7 %collective-permute-start.197 = (bf16[128,2048]{1,0:T(8,128)(2,1)S(1)}, bf16[128,2048]{1,0:T(8,128)(2,1)}, u32[]{:S(2)}, u32[]{:S(2)}) collective-permute-start(bf16[128,2048]{1,0:T(8,128)(2,1)S(1)} %rows_out.3.refs_0_), channel_id=1, source_target_pairs={{0,2},{1,3},{2,0},{3,1},{4,6},{5,7},{6,4},{7,5},{8,10},{9,11},{10,... | collective-permute-start | bytes 1572872 | tf_op jit(solution)/shard_map/ppermute | solution.py:815
  855.5 39.6 %collective-permute-start.198 = (bf16[128,2048]{1,0:T(8,128)(2,1)S(1)}, bf16[128,2048]{1,0:T(8,128)(2,1)}, u32[]{:S(2)}, u32[]{:S(2)}) collective-permute-start(bf16[128,2048]{1,0:T(8,128)(2,1)S(1)} %rows_out.3.refs_0_), channel_id=1, source_target_pairs={{0,1},{1,0},{2,3},{3,2},{4,5},{5,4},{6,7},{7,6},{8,9},{9,8},{10,11... | collective-permute-start | bytes 1572872 | tf_op jit(solution)/shard_map/ppermute | solution.py:815
  856.5 38.6 %collective-permute-start.192 = (bf16[256,1152]{1,0:T(8,128)(2,1)}, bf16[256,1152]{1,0:T(8,128)(2,1)S(1)}, u32[]{:S(2)}, u32[]{:S(2)}) collective-permute-start(bf16[256,1152]{1,0:T(8,128)(2,1)} %add_convert_fusion.2), channel_id=1, source_target_pairs={{0,8},{8,16},{16,24},{24,0},{1,9},{9,17},{17,25},{25,1},{2,10},{10... | collective-permute-start | bytes 1769480 | tf_op jit(solution)/shard_map/ppermute | solution.py:819
  (500 other events, 8882.5 us)
Sparse Core Ops, SparseCore 0:
  485.3 68.7 reduce-scatter.2
  624.7 24.6 reduce-scatter.4
